TPU v7x, 32 devices: a whole 2x2x4 slice. The times are simulated.
32 devices in a mesh: groups: 1, seq: 32 (over z, y, x, core).
Axes of the slice: x: 2, y: 2, z: 4, core: 2. Of those that a mesh axis runs over, the one named last changes fastest.
Arguments:
- query: bfloat16 [4096, 4096], P(('groups', 'seq')), may hold values from -20 to 20
- key: bfloat16 [4096, 512], P(('groups', 'seq')), may hold values from -20 to 20
- value: bfloat16 [4096, 512], P(('groups', 'seq')), may hold values from -6 to 6
- segment_ids: int32 [4096], P(('groups', 'seq')), may hold values from 0 to 15, never falling along the last dimension, each value on 1 to 384 neighbouring positions
- student_rows: bfloat16 [4096, 1536], P(('groups', 'seq')), may hold values from -6 to 6
- projection: bfloat16 [1536, 4096], P('seq'), may hold values from -0.15625 to 0.15625
- send_order: int32 [32, 128], P(('groups', 'seq')), may hold values from 0 to 127, each once within a row
Outputs:
- grad_rows: bfloat16 [4096, 1536], P(('groups', 'seq'))
- grad_proj: float32 [1536, 4096], P(('groups', 'seq'))
Inputs may be any that keep to these rules, and one draw needn't show every extreme that they name: `segment_ids`: ids never fall along the sequence and every id is used; no document is longer than 384 tokens and one has exactly 384. `send_order`: each row is a permutation of the numbers below 128.
All inputs are finite; a program needn't handle non-finite values.
Results may differ from a plain program's by a relative error of at most 0.0045.
Values may be sent and summed in bfloat16 or wider, within the bound.
A program may use at most 192 MiB of HBM per device.

v0:
```python
import jax
import jax.numpy as jnp
from jax import lax
from jax.sharding import PartitionSpec as P

HQ = 32
KVH = 4
HD = 128
REACH = 3


def prefix(value, axis, join, neutral):
    count, mine = (lax.axis_size(axis), lax.axis_index(axis))
    pieces = jax.tree.map(lambda part: lax.all_gather(part, axis), value)
    running = jax.tree.map(
        lambda part, zero: jnp.full_like(part, 0) + jnp.asarray(zero, part.dtype), value, neutral
    )

    def hop(position, running):
        longer = join(running, jax.tree.map(lambda part: part[position], pieces))
        return jax.tree.map(lambda new, old: jnp.where(position < mine, new, old), longer, running)

    return lax.fori_loop(0, count - 1, hop, running)


def shifted(value, axis, steps):
    count = lax.axis_size(axis)
    leading, last = (max(0, -steps), min(count, count - steps))
    return lax.ppermute(value, axis, [(source, source + steps) for source in range(leading, last)])


def combine_runs(early, later):
    first_seg = jnp.where(early[0] < 0, later[0], early[0])
    last_seg = jnp.where(later[0] < 0, early[1], later[1])
    joined = (later[0] == later[1]) & (early[1] == later[1])
    run_start = jnp.where(later[0] < 0, early[2], jnp.where(joined, early[2], later[2]))
    return (first_seg, last_seg, run_start)


def local(query, key, value, segment_ids, student_rows, projection, send_order):
    rows_here = query.shape[0]
    per_group = HQ // KVH
    device_index = lax.axis_index("seq")
    places = device_index * rows_here + jnp.arange(rows_here, dtype=jnp.int32)
    previous = jnp.concatenate([segment_ids[:1] - 1, segment_ids[:-1]])
    boundary = jnp.where(segment_ids != previous, places, -1)
    local_start = lax.cummax(boundary, axis=0)
    summary = (segment_ids[0], segment_ids[-1], local_start[-1])
    identity_runs = (jnp.int32(-1), jnp.int32(-1), jnp.int32(-1))
    before = prefix(summary, "seq", combine_runs, identity_runs)
    doc_start = jnp.where(segment_ids == before[1], before[2], local_start)
    pairs = jnp.concatenate([key, value], axis=1)
    blocks = [pairs]
    for offset in range(1, REACH + 1):
        blocks.append(shifted(pairs, "seq", offset))
    stacked = jnp.stack(blocks, 0)
    block_count = stacked.shape[0]
    offsets = jnp.arange(block_count, dtype=jnp.int32)
    key_places = (
        (device_index - offsets)[:, None] * rows_here
        + jnp.arange(rows_here, dtype=jnp.int32)[None, :]
    ).reshape(block_count * rows_here)
    flat_pairs = stacked.reshape(block_count * rows_here, 2 * KVH * HD)
    allowed = (key_places[None, :] <= places[:, None]) & (key_places[None, :] >= doc_start[:, None])
    score_scale = HD ** (-0.5)
    outputs = []
    for kv_group in range(KVH):
        query_group = query[:, kv_group * per_group * HD : (kv_group + 1) * per_group * HD].reshape(
            rows_here, per_group, HD
        )
        key_group = flat_pairs[:, kv_group * HD : (kv_group + 1) * HD]
        value_group = flat_pairs[:, (KVH + kv_group) * HD : (KVH + kv_group + 1) * HD]
        scores = (
            jnp.einsum("qhd,kd->hqk", query_group, key_group, preferred_element_type=jnp.float32)
            * score_scale
        )
        scores = jnp.where(allowed[None], scores, -jnp.inf)
        row_max = jnp.max(scores, axis=2, keepdims=True)
        weights = jnp.exp(scores - row_max)
        weights = (weights / jnp.sum(weights, axis=2, keepdims=True)).astype(jnp.bfloat16)
        context = jnp.einsum(
            "hqk,kd->qhd", weights, value_group, preferred_element_type=jnp.float32
        )
        outputs.append(context.astype(jnp.bfloat16).reshape(rows_here, per_group * HD))
    teacher = jnp.concatenate(outputs, axis=1)
    outgoing = jnp.take(teacher, send_order[0], axis=0)
    target = lax.all_to_all(outgoing, "seq", split_axis=0, concat_axis=0, tiled=True)
    grad_scale = (rows_here * lax.axis_size("seq")) ** (-0.5)
    full_proj = lax.all_gather(projection, "seq", axis=0, tiled=True)
    predicted = jnp.dot(student_rows, full_proj, preferred_element_type=jnp.float32)
    residual = (predicted - target.astype(jnp.float32)).astype(jnp.bfloat16)
    grad_rows = lax.dot_general(
        residual, full_proj, (((1,), (1,)), ((), ())), preferred_element_type=jnp.float32
    ).astype(jnp.bfloat16)
    partial_term = (
        lax.dot_general(
            student_rows, residual, (((0,), (0,)), ((), ())), preferred_element_type=jnp.float32
        )
        * grad_scale
    )
    grad_proj = lax.psum_scatter(partial_term, "seq", scatter_dimension=0, tiled=True)
    return (grad_rows, grad_proj)


def solution(mesh):
    return jax.shard_map(
        local,
        mesh=mesh,
        in_specs=(
            P(("groups", "seq"), None),
            P(("groups", "seq"), None),
            P(("groups", "seq"), None),
            P(("groups", "seq")),
            P(("groups", "seq"), None),
            P("seq", None),
            P(("groups", "seq"), None),
        ),
        out_specs=(P(("groups", "seq"), None), P(("groups", "seq"), None)),
        check_vma=False,
    )
```

profile of v0, /device:TPU:0, one launch (start us, length us, event | category | flops | bytes accessed | tf_op | source)
XLA Modules:
  0.0 573.7 jit_solution(12513981070151878807)
XLA Ops:
  7.2 0.7 all-gather.3.cloned.1.call-update
  8.0 0.9 constant_dynamic-update-slice_fusion.1
  8.9 0.9 constant_dynamic-update-slice_fusion
  9.8 4.3 collective-permute-start.2
  14.1 4.1 collective-permute-start.1
  18.2 3.0 collective-permute-start
  21.2 1.4 slice_dynamic-update-slice_fusion
  23.3 0.8 fusion.45
  24.9 0.7 bitcast_dynamic-update-slice_fusion
  25.6 0.8 slice_dynamic-update-slice_fusion.1
  26.3 40.4 %all-reduce.3 = (s32[32]{0:T(128)S(1)}, s32[32]{0:T(128)S(1)}, s32[32]{0:T(128)S(1)}) all-reduce(s32[32]{0:T(128)S(1)} %slice_dynamic-update-slice_fusion.1, s32[32]{0:T(128)S(1)} %get-tuple-element.156, s32[32]{0:T(128)S(1)} %bitcast_dynamic-update-slice_fusion), channel_id=1, replica_groups=mesh['groups'=1,'seq'=32] {'seq'}, use_global_device_ids=true, to_apply=%add | all-reduce | flops 96 | bytes 768
  67.3 1.3 reduce.4
  68.8 166.5 %while.15 = (s32[]{:T(128)}, s32[]{:T(128)}, s32[]{:T(128)}, s32[]{:T(128)}, s32[32]{0:T(128)S(1)}, /*index=5*/s32[32]{0:T(128)S(1)}, s32[32]{0:T(128)S(1)}, s32[]{:T(128)}, s32[]{:T(128)}) while((s32[]{:T(128)}, s32[]{:T(128)}, s32[]{:T(128)}, s32[]{:T(128)}, s32[32]{0:T(128)S(1)}, /*index=5*/s32[32]{0:T(128)S(1)}, s32[32]{0:T(128)S(1)}, ...), condition=%wide.region_2.3_spmd, body=%wide.region_1.2_spmd.sunk | while | flops 12 | bytes 241 | solution.py:23
  72.9 0.6 dynamic_slice.26
  74.2 0.6 dynamic_slice.24
  78.3 0.6 dynamic_slice.26
  83.6 0.6 dynamic_slice.26
  89.0 0.6 dynamic_slice.26
  94.4 0.6 dynamic_slice.26
  95.7 0.6 dynamic_slice.24
  99.8 0.6 dynamic_slice.26
  105.1 0.6 dynamic_slice.26
  110.5 0.6 dynamic_slice.26
  115.9 0.6 dynamic_slice.26
  121.2 0.6 dynamic_slice.26
  126.6 0.6 dynamic_slice.26
  132.0 0.6 dynamic_slice.26
  137.4 0.6 dynamic_slice.26
  142.7 0.6 dynamic_slice.26
  148.1 0.6 dynamic_slice.26
  153.5 0.6 dynamic_slice.26
  158.9 0.6 dynamic_slice.26
  164.2 0.6 dynamic_slice.26
  169.6 0.6 dynamic_slice.26
  175.0 0.6 dynamic_slice.26
  180.3 0.6 dynamic_slice.26
  185.7 0.6 dynamic_slice.26
  191.1 0.6 dynamic_slice.26
  196.5 0.6 dynamic_slice.26
  201.8 0.6 dynamic_slice.26
  207.2 0.6 dynamic_slice.26
  212.6 0.6 dynamic_slice.26
  217.9 0.6 dynamic_slice.26
  223.3 0.6 dynamic_slice.26
  228.7 0.6 dynamic_slice.26
  234.1 0.6 dynamic_slice.26
  235.3 0.7 fusion.46
  236.0 1.2 compare_select_fusion.2
  238.3 1.2 pad_maximum_fusion
  239.4 0.8 fusion.63
  240.2 1.0 convolution_convert_fusion.4
  241.4 1.6 fusion.61
  243.0 1.0 convolution_convert_fusion.2
  244.2 0.8 fusion.62
  245.0 1.0 convolution_convert_fusion.3
  246.2 0.8 fusion.60
  247.0 1.0 convolution_convert_fusion.1
  248.3 1.2 gather_fusion
  250.5 30.5 %all_to_all.6 = bf16[32,4,4096]{2,1,0:T(4,128)(2,1)S(1)} all-to-all(bf16[32,4,4096]{2,1,0:T(4,128)(2,1)S(1)} %broadcast_select_fusion), channel_id=1, replica_groups=mesh['groups'=1,'seq'=32] {'seq'}, dimensions={0} | all-to-all | bytes 2097152 | tf_op jit(solution)/shard_map/all_to_all | solution.py:87
  281.2 6.4 %fusion.4 = bf16[128,4096]{1,0:T(8,128)(2,1)S(1)} fusion(f32[128,4096]{1,0:T(8,128)S(1)} %reshape.179, bf16[128,1536]{1,0:T(8,128)(2,1)S(1)} %copy-done, bf16[1536,4096]{1,0:T(8,128)(2,1)} %all-gather.3.cloned.1.call-done), kind=kOutput, calls=%fused_computation.7 | convolution fusion | flops 1611661312 | bytes 16121856 | tf_op jit(solution)/shard_map/dot_general | solution.py:90
  287.5 10.0 %multiply_bitcast_fusion = f32[1536,4096]{0,1:T(8,128)} fusion(bf16[128,4096]{1,0:T(8,128)(2,1)S(1)} %fusion.4, bf16[128,1536]{1,0:T(8,128)(2,1)S(1)} %copy-done), kind=kOutput, calls=%fused_computation.5 | convolution fusion | flops 1616904192 | bytes 26607616 | tf_op jit(solution)/shard_map/dot_general | solution.py:96
  297.6 24.7 %copy.83 = f32[1536,4096]{1,0:T(8,128)} copy(f32[1536,4096]{0,1:T(8,128)} %multiply_bitcast_fusion) | data formatting | bytes 50331648
  322.3 9.7 %convolution_convert_fusion = bf16[128,1536]{1,0:T(8,128)(2,1)} fusion(bf16[128,4096]{1,0:T(8,128)(2,1)S(1)} %fusion.4, bf16[1536,4096]{1,0:T(8,128)(2,1)} %all-gather.3.cloned.1.call-done), kind=kOutput, calls=%fused_computation.8 | convolution fusion | flops 1610809344 | bytes 14024704 | tf_op jit(solution)/shard_map/dot_general | solution.py:92
  332.0 234.9 %reduce-scatter.4.cloned.1.call-done = f32[48,4096]{1,0:T(8,128)} async-done(((f32[1536,4096]{1,0:T(8,128)}), f32[48,4096]{1,0:T(8,128)}) %reduce-scatter.4.cloned.1.call-update) | async-done | bytes 786448
  (106 shorter events, 40.4 us)
Async XLA Ops:
  7.2 274.0 %copy-start = (bf16[128,1536]{1,0:T(8,128)(2,1)S(1)}, bf16[128,1536]{1,0:T(8,128)(2,1)}, u32[]{:S(2)}) copy-start(bf16[128,1536]{1,0:T(8,128)(2,1)} %param.13) | copy-start | bytes 1179652
  7.2 230.1 %copy-start.2 = (bf16[128,4096]{1,0:T(8,128)(2,1)S(1)}, bf16[128,4096]{1,0:T(8,128)(2,1)}, u32[]{:S(2)}) copy-start(bf16[128,4096]{1,0:T(8,128)(2,1)} %param.9) | copy-start | bytes 3145732
  7.2 273.9 %all-gather.3.cloned.1.call-start = ((), (), s32[]{:S(2)}) async-start(), calls=%async_computation.2 | async-start | bytes 12976128 | tf_op jit(solution)/shard_map/all_gather | solution.py:89
  7.9 559.0 %reduce-scatter.4.cloned.1.call-start = ((), (), s32[]{:S(2)}) async-start(), calls=%async_computation.3 | async-start | bytes 25952256
  9.8 228.4 %collective-permute-start.2 = (bf16[128,1024]{1,0:T(8,128)(2,1)S(1)}, bf16[128,1024]{1,0:T(8,128)(2,1)S(1)}, u32[]{:S(2)}, u32[]{:S(2)}) collective-permute-start(bf16[128,1024]{1,0:T(8,128)(2,1)S(1)} %constant_dynamic-update-slice_fusion), channel_id=1, source_target_pairs={{0,3},{1,4},{2,5},{3,6},{4,7},{5,8},{6,9},{7,10},{8,11},{9,12},{10... | collective-permute-start | bytes 786440 | tf_op jit(solution)/shard_map/ppermute | solution.py:29
  14.1 224.1 %collective-permute-start.1 = (bf16[128,1024]{1,0:T(8,128)(2,1)S(1)}, bf16[128,1024]{1,0:T(8,128)(2,1)}, u32[]{:S(2)}, u32[]{:S(2)}) collective-permute-start(bf16[128,1024]{1,0:T(8,128)(2,1)S(1)} %constant_dynamic-update-slice_fusion), channel_id=1, source_target_pairs={{0,2},{1,3},{2,4},{3,5},{4,6},{5,7},{6,8},{7,9},{8,10},{9,11},{10,... | collective-permute-start | bytes 786440 | tf_op jit(solution)/shard_map/ppermute | solution.py:29
  18.2 220.1 %collective-permute-start = (bf16[128,1024]{1,0:T(8,128)(2,1)S(1)}, bf16[128,1024]{1,0:T(8,128)(2,1)}, u32[]{:S(2)}, u32[]{:S(2)}) collective-permute-start(bf16[128,1024]{1,0:T(8,128)(2,1)S(1)} %constant_dynamic-update-slice_fusion), channel_id=1, source_target_pairs={{0,1},{1,2},{2,3},{3,4},{4,5},{5,6},{6,7},{7,8},{8,9},{9,10},{10,1... | collective-permute-start | bytes 786440 | tf_op jit(solution)/shard_map/ppermute | solution.py:29
  237.3 0.7 copy-start.5
  238.2 3.0 copy-start.3
  241.3 1.8 copy-start.4
  322.3 244.6 %copy-start.1 = (bf16[128,1536]{1,0:T(8,128)(2,1)S(1)}, bf16[128,1536]{1,0:T(8,128)(2,1)}, u32[]{:S(2)}) copy-start(bf16[128,1536]{1,0:T(8,128)(2,1)} %param.13) | copy-start | bytes 1179652
Sparse Core Ops, SparseCore 0:
  10.9 103.6 all-gather.2
  322.4 244.4 reduce-scatter.3
where the time goes:
time: 576 us; the launch traced here: 574 us
  waiting for transfers between devices  236 us (41%)
  loops' own time  110 us (19%)
  local copies, waits for them, and re-layouts  90.2 us (16%)
  blocking collectives  70.9 us (12%)
  matrix products  34.2 us (6%)
  between operations  15 us (3%)
  starting transfers between devices  11.5 us (2%)
  other arithmetic  6.22 us (1%)
    unnamed x3, waiting for transfers between devices  236 us
    another operation x1, loops' own time, prefix(): return lax.fori_loop(0, count - 1, hop, running)  110 us
    dynamic_slice x93, local copies, waits for them, and re-layouts, hop(): longer = join(running, jax.tree.map(lambda part: part[position], pieces))  56.4 us
    unnamed x1, blocking collectives  40.4 us
    all_to_all x1, blocking collectives, local(): lax.all_to_all(outgoing, 'seq', split_axis=0, concat_axis=0, tiled=True)  30.5 us
    unnamed x25, local copies, waits for them, and re-layouts  29.7 us
  transfers between devices with their start and end apart: 5, of which 1 were waited for; matrix products, arithmetic and copies ran while one was open for 16% of the time, Pallas kernels for 0%

commit v1 on v0

v1 whole, which is shorter than its diff:
```python
import jax
import jax.numpy as jnp
from jax import lax
from jax.sharding import PartitionSpec as P

HQ = 32
KVH = 4
HD = 128
REACH = 3
COLS = 8


def shifted(value, axis, steps):
    count = lax.axis_size(axis)
    return lax.ppermute(value, axis, [(s, s + steps) for s in range(count - steps)])


def attention(query, key, value, segment_ids):
    rows = query.shape[0]
    per_group = HQ // KVH
    me = lax.axis_index("seq")
    ids = jnp.broadcast_to(segment_ids.astype(jnp.bfloat16)[:, None], (rows, HD))
    block = jnp.concatenate([key, value, ids], axis=1)
    blocks = [block] + [shifted(block, "seq", step) for step in range(1, REACH + 1)]
    flat = jnp.concatenate(blocks[::-1], axis=0)
    span = flat.shape[0]
    key_ids = flat[:, 2 * KVH * HD].astype(jnp.int32)
    places = jnp.arange(rows, dtype=jnp.int32) + REACH * rows
    key_places = jnp.arange(span, dtype=jnp.int32)
    allowed = (
        (key_places[None, :] <= places[:, None])
        & (key_ids[None, :] == segment_ids[:, None])
        & (key_places[None, :] >= (REACH - me) * rows)
    )
    scale = HD ** (-0.5)
    outputs = []
    for g in range(KVH):
        q = query[:, g * per_group * HD : (g + 1) * per_group * HD].reshape(rows, per_group, HD)
        k = flat[:, g * HD : (g + 1) * HD]
        v = flat[:, (KVH + g) * HD : (KVH + g + 1) * HD]
        scores = jnp.einsum("qhd,kd->hqk", q, k, preferred_element_type=jnp.float32) * scale
        scores = jnp.where(allowed[None], scores, -jnp.inf)
        top = jnp.max(scores, axis=2, keepdims=True)
        weights = jnp.exp(scores - top)
        weights = (weights / jnp.sum(weights, axis=2, keepdims=True)).astype(jnp.bfloat16)
        context = jnp.einsum("hqk,kd->qhd", weights, v, preferred_element_type=jnp.float32)
        outputs.append(context.astype(jnp.bfloat16).reshape(rows, per_group * HD))
    return jnp.concatenate(outputs, axis=1)


def local(query, key, value, segment_ids, student_rows, projection, send_order):
    rows = query.shape[0]
    n = lax.axis_size("seq")
    cols = COLS
    bands = n // cols
    width = HQ * HD // cols
    depth = projection.shape[0]
    ds = student_rows.shape[1]
    share = rows // n
    near = [[b * cols + c for c in range(cols)] for b in range(bands)]
    far = [[b * cols + c for b in range(bands)] for c in range(cols)]

    band_rows = lax.all_gather(student_rows, "seq", axis=0, tiled=True, axis_index_groups=near)
    pieces = projection.reshape(depth, cols, width).transpose(1, 0, 2)
    pieces = lax.all_to_all(
        pieces, "seq", split_axis=0, concat_axis=0, tiled=True, axis_index_groups=near
    )
    column = lax.all_gather(
        pieces.reshape(cols * depth, width), "seq", axis=0, tiled=True, axis_index_groups=far
    )
    teacher = attention(query, key, value, segment_ids)
    outgoing = jnp.take(teacher, send_order[0], axis=0)
    outgoing = outgoing.reshape(bands, cols * share, cols, width).transpose(0, 2, 1, 3)
    arrived = lax.all_to_all(
        outgoing.reshape(n, cols * share, width), "seq", split_axis=0, concat_axis=0, tiled=True
    )
    target = arrived.reshape(n, cols, share, width).transpose(1, 0, 2, 3).reshape(cols * rows, width)
    predicted = jnp.dot(band_rows, column, preferred_element_type=jnp.float32)
    residual = (predicted - target.astype(jnp.float32)).astype(jnp.bfloat16)
    proj_part = lax.dot_general(
        band_rows, residual, (((0,), (0,)), ((), ())), preferred_element_type=jnp.float32
    ).astype(jnp.bfloat16)
    proj_parts = lax.all_to_all(
        proj_part.reshape(n, depth, width), "seq", split_axis=0, concat_axis=0, tiled=True
    )
    rows_part = lax.dot_general(
        residual, column, (((1,), (1,)), ((), ())), preferred_element_type=jnp.float32
    ).astype(jnp.bfloat16)
    rows_parts = lax.all_to_all(
        rows_part.reshape(cols, rows, ds),
        "seq", split_axis=0, concat_axis=0, tiled=True, axis_index_groups=near,
    )
    grad_rows = jnp.sum(rows_parts.astype(jnp.float32), axis=0).astype(jnp.bfloat16)
    grad_scale = (rows * n) ** (-0.5)
    summed = jnp.sum(proj_parts.reshape(bands, cols, depth, width).astype(jnp.float32), axis=0)
    grad_proj = (summed * grad_scale).transpose(1, 0, 2).reshape(depth, cols * width)
    return (grad_rows, grad_proj)


def solution(mesh):
    both = ("groups", "seq")
    return jax.shard_map(
        local,
        mesh=mesh,
        in_specs=(
            P(both, None), P(both, None), P(both, None), P(both), P(both, None),
            P("seq", None), P(both, None),
        ),
        out_specs=(P(both, None), P(both, None)),
        check_vma=False,
    )
```

time: 576 us -> 219 us (0.38)
  waiting for transfers between devices: 236 us -> 69.8 us
  loops' own time: 110 us -> 0 us
  local copies, waits for them, and re-layouts: 90.2 us -> 15.2 us
  matrix products: 34.2 us -> 21.9 us
    unnamed x3 -> x2, waiting for transfers between devices: 236 us -> 0.03 us
    another operation x1 -> x0, loops' own time: 110 us -> none  [prefix(): return lax.fori_loop(0, count - 1, hop, running)]
    all_to_all x0 -> x2, waiting for transfers between devices: none -> 65.6 us  [the longest x1 36.5 us: local(): lax.all_to_all(proj_part.reshape(n, depth, width), 'seq', split_axis=0, c...]
    dynamic_slice x93 -> x0, local copies, waits for them, and re-layouts: 56.4 us -> none  [hop(): longer = join(running, jax.tree.map(lambda part: part[position], pieces))]
    all_to_all x1 -> x2, blocking collectives: 30.5 us -> 75.5 us  [the longest x1 62.1 us: local(): lax.all_to_all(outgoing.reshape(n, cols * share, width), 'seq', split_axi...]
    unnamed x1 -> x0, blocking collectives: 40.4 us -> none
    unnamed x25 -> x29, local copies, waits for them, and re-layouts: 29.7 us -> 4.22 us
    dot_general x7, matrix products: 30.3 us -> 18.9 us  [the longest x1 6.24 us: local(): lax.dot_general(band_rows, residual, (((0,), (0,)), ((), ())), preferred_...]
  transfers between devices with their start and end apart: 5 -> 7, of which waited for: 1 -> 4; matrix products, arithmetic and copies ran while one was open for 16% -> 14% of each run, Pallas kernels for 0% -> 0%
where the time goes in v1:
time: 219 us; the launch traced here: 218 us
  blocking collectives  75.5 us (34%)
  waiting for transfers between devices  69.8 us (32%)
  matrix products  21.9 us (10%)
  local copies, waits for them, and re-layouts  15.2 us (7%)
  starting transfers between devices  14.9 us (7%)
  between operations  14.4 us (7%)
  other arithmetic  6.53 us (3%)
    all_to_all x1, blocking collectives, local(): lax.all_to_all(outgoing.reshape(n, cols * share, width), 'seq', split_axi...  62.1 us
    all_to_all x1, waiting for transfers between devices, local(): lax.all_to_all(proj_part.reshape(n, depth, width), 'seq', split_axis=0, c...  36.5 us
    all_to_all x1, waiting for transfers between devices, local(): lax.all_to_all(rows_part.reshape(cols, rows, ds), 'seq', split_axis=0, co...  29 us
    all_to_all x1, blocking collectives, local(): lax.all_to_all(pieces, 'seq', split_axis=0, concat_axis=0, tiled=True, ax...  13.4 us
    ppermute x3, starting transfers between devices, shifted(): lax.ppermute(value, axis, [(s, s + steps) for s in range(count - steps)])  7.75 us
    dot_general x1, matrix products, local(): lax.dot_general(band_rows, residual, (((0,), (0,)), ((), ())), preferred_...  6.24 us
    convert_element_type x3, local copies, waits for them, and re-layouts, local(): residual = (predicted - target.astype(jnp.float32)).astype(jnp.bfloat16)  5.31 us
    dot_general x1, matrix products, local(): predicted = jnp.dot(band_rows, column, preferred_element_type=jnp.float32)  4.87 us
  transfers between devices with their start and end apart: 7, of which 4 were waited for; matrix products, arithmetic and copies ran while one was open for 14% of the time, Pallas kernels for 0%

profile of v1, /device:TPU:0, one launch (start us, length us, event | category | flops | bytes accessed | tf_op | source)
XLA Modules:
  0.0 218.3 jit_solution(16276587137259497606)
XLA Ops:
  7.2 0.0 all-gather.5.cloned.1.call-start
  7.3 1.2 copy.142
  8.5 0.1 copy.95
  8.6 13.4 %all_to_all.20 = bf16[8,48,512]{2,1,0:T(8,128)(2,1)} all-to-all(bf16[8,48,512]{2,1,0:T(8,128)(2,1)S(1)} %copy.95), channel_id=1, replica_groups={{0,1,2,3,4,5,6,7},{8,9,10,11,12,13,14,15},{16,17,18,19,20,21,22,23},{24..., dimensions={0} | all-to-all | bytes 786432 | tf_op jit(solution)/shard_map/all_to_all | solution.py:65
  22.0 0.0 all-gather.5.cloned.1.call-update
  22.1 0.0 all-gather.3.cloned.1.call-start
  22.1 0.1 broadcast_in_dim.58
  22.2 0.7 pad_maximum_fusion.1
  23.0 1.5 collective-permute-start.2
  24.5 2.8 %collective-permute-start.1 = (bf16[128,1152]{1,0:T(8,128)(2,1)}, bf16[128,1152]{1,0:T(8,128)(2,1)S(1)}, u32[]{:S(2)}, u32[]{:S(2)}) collective-permute-start(bf16[128,1152]{1,0:T(8,128)(2,1)} %pad_maximum_fusion.1), channel_id=1, source_target_pairs={{0,2},{1,3},{2,4},{3,5},{4,6},{5,7},{6,8},{7,9},{8,10},{9,11},{10,... | collective-permute-start | bytes 884744 | tf_op jit(solution)/shard_map/ppermute | solution.py:15
  27.4 3.4 %collective-permute-start = (bf16[128,1152]{1,0:T(8,128)(2,1)}, bf16[128,1152]{1,0:T(8,128)(2,1)S(1)}, u32[]{:S(2)}, u32[]{:S(2)}) collective-permute-start(bf16[128,1152]{1,0:T(8,128)(2,1)} %pad_maximum_fusion.1), channel_id=1, source_target_pairs={{0,3},{1,4},{2,5},{3,6},{4,7},{5,8},{6,9},{7,10},{8,11},{9,12},{10... | collective-permute-start | bytes 884744 | tf_op jit(solution)/shard_map/ppermute | solution.py:15
  30.8 0.0 all-gather.3.cloned.1.call-update
  30.8 0.5 iota_add_fusion
  31.3 0.5 broadcast.146
  31.8 0.7 reduce.6
  32.5 0.1 squeeze.6
  32.6 0.1 fusion.60
  32.7 0.9 copy.137
  33.5 0.8 copy.139
  34.4 0.2 copy.138
  34.5 0.2 copy.140
  34.7 0.0 collective-permute-done.2
  34.8 0.4 collective-permute-done.1
  35.1 3.8 %collective-permute-done = bf16[128,1152]{1,0:T(8,128)(2,1)S(1)} collective-permute-done((bf16[128,1152]{1,0:T(8,128)(2,1)}, bf16[128,1152]{1,0:T(8,128)(2,1)S(1)}, u32[]{:S(2)}, u32[]{:S(2)}) %collective-permute-start) | collective-permute-done | bytes 294944 | tf_op jit(solution)/shard_map/ppermute | solution.py:15
  38.9 0.1 maximum_maximum_fusion
  39.0 0.1 convert_reduce_fusion.1
  39.1 0.8 fusion.22
  40.0 0.8 fusion.64
  40.7 0.0 copy-start.5
  40.7 1.0 convolution_convert_fusion.5
  41.8 0.1 copy.112
  41.9 0.0 copy-done.5
  42.0 0.8 fusion.62
  42.7 1.0 convolution_convert_fusion.3
  43.8 0.1 copy.114
  43.9 0.8 fusion.63
  44.7 1.0 convolution_convert_fusion.4
  45.7 0.1 copy.113
  45.9 0.8 fusion.61
  46.7 1.0 convolution_convert_fusion.2
  47.7 0.1 copy.115
  47.9 0.1 pad_maximum_fusion
  47.9 1.2 gather_fusion
  49.1 0.4 copy.143
  49.5 0.4 copy_select_fusion
  49.9 62.1 %all_to_all.21 = bf16[32,32,512]{2,1,0:T(8,128)(2,1)S(1)} all-to-all(bf16[32,32,512]{2,1,0:T(8,128)(2,1)S(1)} %bitcast.168), channel_id=1, replica_groups=mesh['groups'=1,'seq'=32] {'seq'}, dimensions={0} | all-to-all | bytes 2097152 | tf_op jit(solution)/shard_map/all_to_all | solution.py:74
  112.0 0.6 copy.117
  112.6 2.7 %copy.118 = f32[8,32,4,512]{3,2,1,0:T(4,128)} copy(f32[8,32,4,512]{3,1,2,0:T(8,128)S(1)} %bitcast.164) | data formatting | bytes 4194304 | tf_op jit(solution)/shard_map/convert_element_type | solution.py:79
  115.3 2.0 reshape.197
  117.3 0.0 all-gather.5.cloned.1.call-done
  117.3 0.0 all-gather.3.cloned.1.call-done
  117.4 4.9 %fusion.65 = f32[1024,512]{1,0:T(8,128)S(1)} fusion(bf16[1024,1536]{1,0:T(8,128)(2,1)} %all-gather.3.cloned.1.call-done, bf16[1536,512]{1,0:T(8,128)(2,1)} %all-gather.5.cloned.1.call-done), kind=kOutput, calls=%fused_computation.95 | convolution fusion | flops 1610612736 | bytes 6815744 | tf_op jit(solution)/shard_map/dot_general | solution.py:78
  122.2 0.0 copy-done
  122.3 3.6 %convolution_convert_fusion = bf16[1024,1536]{1,0:T(8,128)(2,1)} fusion(bf16[1536,512]{1,0:T(8,128)(2,1)S(1)} %copy-done.9, f32[1024,512]{1,0:T(8,128)S(1)} %fusion.65, f32[1024,512]{1,0:T(8,128)S(1)} %reshape.197), kind=kOutput, calls=%fused_computation.5 | convolution fusion | flops 1613234176 | bytes 8912896 | tf_op jit(solution)/shard_map/dot_general | solution.py:86
  125.9 3.7 %all-to-all-start.2 = ((bf16[8,128,1536]{2,1,0:T(8,128)(2,1)}), bf16[8,128,1536]{2,1,0:T(8,128)(2,1)S(1)}, u32[]{:S(2)}, u32[]{:S(2)}) async-start(bf16[8,128,1536]{2,1,0:T(8,128)(2,1)} %bitcast.169), calls=%async_computation.2 | async-start | bytes 6291456 | tf_op jit(solution)/shard_map/all_to_all | solution.py:89
  129.5 6.2 %fusion.4 = bf16[1536,512]{0,1:T(8,128)(2,1)} fusion(bf16[1024,1536]{1,0:T(8,128)(2,1)} %all-gather.3.cloned.1.call-done, f32[1024,512]{1,0:T(8,128)} %copy-done.1, f32[1024,512]{1,0:T(8,128)} %copy-done), kind=kOutput, calls=%fused_computation.8 | convolution fusion | flops 1612447744 | bytes 8912896 | tf_op jit(solution)/shard_map/dot_general | solution.py:80
  135.8 2.6 %copy.119 = bf16[1536,512]{1,0:T(8,128)(2,1)} copy(bf16[1536,512]{0,1:T(8,128)(2,1)} %fusion.4) | data formatting | bytes 3145728 | tf_op jit(solution)/shard_map/convert_element_type | solution.py:82
  138.4 29.0 %all-to-all-done.2 = bf16[8,128,1536]{2,1,0:T(8,128)(2,1)S(1)} async-done(((bf16[8,128,1536]{2,1,0:T(8,128)(2,1)}), bf16[8,128,1536]{2,1,0:T(8,128)(2,1)S(1)}, u32[]{:S(2)}, u32[]{:S(2)}) %all-to-all-start.2) | async-done | bytes 3145760 | tf_op jit(solution)/shard_map/all_to_all | solution.py:89
  167.4 3.4 %all-to-all-start.3 = ((bf16[32,48,512]{2,1,0:T(8,128)(2,1)}), bf16[32,48,512]{2,1,0:T(8,128)(2,1)}, u32[]{:S(2)}, u32[]{:S(2)}) async-start(bf16[32,48,512]{2,1,0:T(8,128)(2,1)} %bitcast.165), calls=%async_computation.3 | async-start | bytes 3145728 | tf_op jit(solution)/shard_map/all_to_all | solution.py:83
  170.8 1.3 reduce_sum.61
  172.1 36.5 %all-to-all-done.3 = bf16[32,48,512]{2,1,0:T(8,128)(2,1)} async-done(((bf16[32,48,512]{2,1,0:T(8,128)(2,1)}), bf16[32,48,512]{2,1,0:T(8,128)(2,1)}, u32[]{:S(2)}, u32[]{:S(2)}) %all-to-all-start.3) | async-done | bytes 1572896 | tf_op jit(solution)/shard_map/all_to_all | solution.py:83
  208.7 1.8 convert_reduce_fusion
  210.4 0.1 multiply_bitcast_fusion
  210.5 0.9 copy.141
  (24 shorter events, 0.1 us)
Async XLA Ops:
  7.2 14.9 %copy-start.8 = (s32[128]{0:T(128)S(1)}, s32[128]{0:T(128)}, u32[]{:S(2)}) copy-start(s32[128]{0:T(128)} %param.10) | copy-start | bytes 1540
  7.2 15.0 %copy-start.3 = (bf16[128,512]{1,0:T(8,128)(2,1)S(1)}, bf16[128,512]{1,0:T(8,128)(2,1)}, u32[]{:S(2)}) copy-start(bf16[128,512]{1,0:T(8,128)(2,1)} %param.9) | copy-start | bytes 393220
  7.2 15.0 %copy-start.4 = (bf16[128,512]{1,0:T(8,128)(2,1)S(1)}, bf16[128,512]{1,0:T(8,128)(2,1)}, u32[]{:S(2)}) copy-start(bf16[128,512]{1,0:T(8,128)(2,1)} %param.8) | copy-start | bytes 393220
  7.2 24.1 %copy-start.10 = (s32[1,128]{1,0:T(1,128)S(1)}, s32[1,128]{1,0:T(1,128)}, u32[]{:S(2)}) copy-start(s32[1,128]{1,0:T(1,128)} %param.13) | copy-start | bytes 1540
  7.2 25.4 %copy-start.2 = (bf16[128,4096]{1,0:T(8,128)(2,1)S(1)}, bf16[128,4096]{1,0:T(8,128)(2,1)}, u32[]{:S(2)}) copy-start(bf16[128,4096]{1,0:T(8,128)(2,1)} %param.7) | copy-start | bytes 3145732
  7.2 110.1 %all-gather.5.cloned.1.call-start = ((), (), s32[]{:S(2)}) async-start(), calls=%async_computation.5 | async-start | bytes 1966080 | tf_op jit(solution)/shard_map/all_gather | solution.py:68
  22.1 95.3 %all-gather.3.cloned.1.call-start = ((), (), s32[]{:S(2)}) async-start(), calls=%async_computation.4 | async-start | bytes 3538944 | tf_op jit(solution)/shard_map/all_gather | solution.py:63
  23.0 11.8 %collective-permute-start.2 = (bf16[128,1152]{1,0:T(8,128)(2,1)}, bf16[128,1152]{1,0:T(8,128)(2,1)S(1)}, u32[]{:S(2)}, u32[]{:S(2)}) collective-permute-start(bf16[128,1152]{1,0:T(8,128)(2,1)} %pad_maximum_fusion.1), channel_id=1, source_target_pairs={{0,1},{1,2},{2,3},{3,4},{4,5},{5,6},{6,7},{7,8},{8,9},{9,10},{10,1... | collective-permute-start | bytes 884744 | tf_op jit(solution)/shard_map/ppermute | solution.py:15
  24.5 10.6 %collective-permute-start.1 = (bf16[128,1152]{1,0:T(8,128)(2,1)}, bf16[128,1152]{1,0:T(8,128)(2,1)S(1)}, u32[]{:S(2)}, u32[]{:S(2)}) collective-permute-start(bf16[128,1152]{1,0:T(8,128)(2,1)} %pad_maximum_fusion.1), channel_id=1, source_target_pairs={{0,2},{1,3},{2,4},{3,5},{4,6},{5,7},{6,8},{7,9},{8,10},{9,11},{10,... | collective-permute-start | bytes 884744 | tf_op jit(solution)/shard_map/ppermute | solution.py:15
  27.4 11.5 %collective-permute-start = (bf16[128,1152]{1,0:T(8,128)(2,1)}, bf16[128,1152]{1,0:T(8,128)(2,1)S(1)}, u32[]{:S(2)}, u32[]{:S(2)}) collective-permute-start(bf16[128,1152]{1,0:T(8,128)(2,1)} %pad_maximum_fusion.1), channel_id=1, source_target_pairs={{0,3},{1,4},{2,5},{3,6},{4,7},{5,8},{6,9},{7,10},{8,11},{9,12},{10... | collective-permute-start | bytes 884744 | tf_op jit(solution)/shard_map/ppermute | solution.py:15
  34.5 5.4 %copy-start.6 = (bf16[128,1024]{0,1:T(8,128)(2,1)S(1)}, bf16[128,1024]{0,1:T(8,128)(2,1)}, u32[]{:S(2)}) copy-start(bf16[128,1024]{0,1:T(8,128)(2,1)} %copy.137) | copy-start | bytes 786436
  39.0 1.7 copy-start.7
  40.7 1.2 copy-start.5
  117.3 4.9 %copy-start = (f32[1024,512]{1,0:T(8,128)}, f32[1024,512]{1,0:T(8,128)S(1)}, u32[]{:S(2)}) copy-start(f32[1024,512]{1,0:T(8,128)S(1)} %reshape.197) | copy-start | bytes 6291460
  117.3 4.9 %copy-start.9 = (bf16[1536,512]{1,0:T(8,128)(2,1)S(1)}, bf16[1536,512]{1,0:T(8,128)(2,1)}, u32[]{:S(2)}) copy-start(bf16[1536,512]{1,0:T(8,128)(2,1)} %all-gather.5.cloned.1.call-done) | copy-start | bytes 4718596
  122.2 3.6 %copy-start.1 = (f32[1024,512]{1,0:T(8,128)}, f32[1024,512]{1,0:T(8,128)S(1)}, u32[]{:S(2)}) copy-start(f32[1024,512]{1,0:T(8,128)S(1)} %fusion.65) | copy-start | bytes 6291460
  125.9 41.6 %all-to-all-start.2 = ((bf16[8,128,1536]{2,1,0:T(8,128)(2,1)}), bf16[8,128,1536]{2,1,0:T(8,128)(2,1)S(1)}, u32[]{:S(2)}, u32[]{:S(2)}) async-start(bf16[8,128,1536]{2,1,0:T(8,128)(2,1)} %bitcast.169), calls=%async_computation.2 | async-start | bytes 6291456 | tf_op jit(solution)/shard_map/all_to_all | solution.py:89
  167.4 41.3 %all-to-all-start.3 = ((bf16[32,48,512]{2,1,0:T(8,128)(2,1)}), bf16[32,48,512]{2,1,0:T(8,128)(2,1)}, u32[]{:S(2)}, u32[]{:S(2)}) async-start(bf16[32,48,512]{2,1,0:T(8,128)(2,1)} %bitcast.165), calls=%async_computation.3 | async-start | bytes 3145728 | tf_op jit(solution)/shard_map/all_to_all | solution.py:83
Sparse Core Ops, SparseCore 0:
  22.2 36.4 all-gather.4
  60.6 49.2 all-gather.2

commit v2 on v1

v2 whole, which is shorter than its diff:
```python
import functools

import jax
import jax.numpy as jnp
from jax import lax
from jax.experimental import pallas as pl
from jax.experimental.pallas import tpu as pltpu
from jax.sharding import PartitionSpec as P

HQ = 32
KVH = 4
HD = 128
REACH = 3
COLS = 8
MESH = pl.DeviceIdType.MESH


def reach_kernel(n, seg_ref, segcol_ref, order_ref, query_ref, pairs_ref, rows_ref, proj_ref,
                 band_ref, column_ref, arrived_ref, pairs_in, ids_in, outgoing,
                 pair_send, pair_recv, id_send, id_recv, col_send, col_recv,
                 row_send, row_recv, out_send, out_recv, own_sem):
    me = lax.axis_index("seq")
    cols = COLS
    bands = n // cols
    my_band, my_col = me // cols, me % cols
    rows = query_ref.shape[0]
    width = HQ * HD // cols
    heads = HQ // cols

    def remote(src, dst, send, recv, peer):
        return pltpu.make_async_remote_copy(
            src_ref=src, dst_ref=dst, send_sem=send, recv_sem=recv,
            device_id={"seq": peer}, device_id_type=MESH)

    def pair_copy(k):
        return remote(pairs_ref, pairs_in.at[k - 1], pair_send.at[k - 1], pair_recv.at[k - 1], (me + k) % n)

    def id_copy(k):
        return remote(seg_ref, ids_in.at[k - 1], id_send.at[k - 1], id_recv.at[k - 1], (me + k) % n)

    def col_copy(peer, slot, place):
        block = proj_ref.at[:, pl.ds(pl.multiple_of((peer % cols) * width, width), width)]
        return remote(block, column_ref.at[place], col_send.at[slot], col_recv.at[place], peer)

    def row_copy(peer, slot, place):
        return remote(rows_ref, band_ref.at[place], row_send.at[slot], row_recv.at[place], peer)

    def out_copy(peer, place):
        return remote(outgoing.at[peer % cols, peer // cols], arrived_ref.at[place],
                      out_send.at[peer], out_recv.at[place], peer)

    own = [
        pltpu.make_async_copy(rows_ref, band_ref.at[my_col], own_sem.at[0]),
        pltpu.make_async_copy(
            proj_ref.at[:, pl.ds(pl.multiple_of(my_col * width, width), width)],
            column_ref.at[me], own_sem.at[1]),
        pltpu.make_async_copy(outgoing.at[my_col, my_band], arrived_ref.at[me], own_sem.at[2]),
    ]

    barrier = pltpu.get_barrier_semaphore()

    @pl.loop(1, n)
    def _(k):
        pl.semaphore_signal(barrier, inc=1, device_id={"seq": (me + k) % n}, device_id_type=MESH)

    pl.semaphore_wait(barrier, n - 1)
    for k in range(1, REACH + 1):
        id_copy(k).start()
        pair_copy(k).start()
    own[0].start()
    own[1].start()

    @pl.loop(1, cols)
    def _(k):
        row_copy(my_band * cols + (my_col + k) % cols, k, my_col).start()

    @pl.loop(1, n)
    def _(k):
        col_copy((me + k) % n, k, me).start()

    for k in range(1, REACH + 1):
        id_copy(k).wait()
        pair_copy(k).wait()

    key_ids = jnp.concatenate([seg_ref[0:1, :]] + [ids_in[k, 0:1, :] for k in range(REACH)], axis=1)
    span = (REACH + 1) * rows
    place = lax.broadcasted_iota(jnp.int32, (rows, span), 1)
    back = place // rows
    at = place - 2 * rows * back
    row = lax.broadcasted_iota(jnp.int32, (rows, span), 0)
    allowed = (at <= row) & (key_ids == segcol_ref[:, 0:1]) & (back <= me)
    bias = jnp.where(allowed, 0.0, -jnp.inf).astype(jnp.float32)
    pick = (lax.broadcasted_iota(jnp.int32, (rows, rows), 1) == order_ref[:, 0:1]).astype(jnp.bfloat16)
    per_group = HQ // KVH
    trans = (((1,), (1,)), ((), ()))

    @pl.loop(0, cols)
    def _(c):
        g = (c * heads) // per_group
        kcol = pl.ds(pl.multiple_of(g * HD, HD), HD)
        vcol = pl.ds(pl.multiple_of((KVH + g) * HD, HD), HD)
        keys = jnp.concatenate([pairs_ref[:, kcol]] + [pairs_in[k, :, kcol] for k in range(REACH)], axis=0)
        values = jnp.concatenate([pairs_ref[:, vcol]] + [pairs_in[k, :, vcol] for k in range(REACH)], axis=0)
        made = []
        for h in range(heads):
            q = query_ref[:, pl.ds(pl.multiple_of(c * width + h * HD, HD), HD)]
            scores = lax.dot_general(q, keys, trans, preferred_element_type=jnp.float32)
            scores = scores * (HD ** -0.5) + bias
            top = jnp.max(scores, axis=1, keepdims=True)
            weights = jnp.exp(scores - top)
            weights = (weights / jnp.sum(weights, axis=1, keepdims=True)).astype(jnp.bfloat16)
            made.append(jnp.dot(weights, values, preferred_element_type=jnp.float32).astype(jnp.bfloat16))
        teacher = jnp.concatenate(made, axis=1)
        ordered = jnp.dot(pick, teacher, preferred_element_type=jnp.float32)
        outgoing[c] = ordered.reshape(bands, rows // bands, width).astype(jnp.bfloat16)

        @pl.loop(0, bands)
        def _(b):
            peer = b * cols + c

            @pl.when(peer != me)
            def _():
                out_copy(peer, me).start()

    own[2].start()
    for copy in own:
        copy.wait()

    @pl.loop(1, cols)
    def _(k):
        row_copy(my_band * cols + (my_col + k) % cols, k, (my_col + cols - k) % cols).wait()

    @pl.loop(1, n)
    def _(k):
        col_copy((me + k) % n, k, (me + n - k) % n).wait()
        out_copy((me + k) % n, (me + n - k) % n).wait()


def exchange(query, pairs, segment_ids, student_rows, projection, send_order):
    n = lax.axis_size("seq")
    rows = query.shape[0]
    depth = projection.shape[0]
    width = HQ * HD // COLS
    bands = n // COLS
    seg = jnp.broadcast_to(segment_ids[None, :], (8, rows))
    segcol = jnp.broadcast_to(segment_ids[:, None], (rows, HD))
    order = jnp.broadcast_to(send_order[0][:, None], (rows, HD))
    vmem = pl.BlockSpec(memory_space=pltpu.VMEM)
    hbm = pl.BlockSpec(memory_space=pl.ANY)
    dma = pltpu.SemaphoreType.DMA
    bf16 = jnp.bfloat16
    return pl.pallas_call(
        functools.partial(reach_kernel, n),
        out_shape=(
            jax.ShapeDtypeStruct((COLS, rows, student_rows.shape[1]), bf16),
            jax.ShapeDtypeStruct((n, depth, width), bf16),
            jax.ShapeDtypeStruct((n, rows // bands, width), bf16),
        ),
        in_specs=[vmem] * 5 + [hbm] * 2,
        out_specs=(hbm, hbm, hbm),
        scratch_shapes=[
            pltpu.VMEM((REACH, rows, pairs.shape[1]), bf16),
            pltpu.VMEM((REACH, 8, rows), jnp.int32),
            pltpu.VMEM((COLS, bands, rows // bands, width), bf16),
            dma((REACH,)), dma((REACH,)), dma((REACH,)), dma((REACH,)),
            dma((n,)), dma((n,)), dma((COLS,)), dma((COLS,)), dma((n,)), dma((n,)), dma((3,)),
        ],
        compiler_params=pltpu.CompilerParams(
            collective_id=0, has_side_effects=True, vmem_limit_bytes=40 * 1024 * 1024),
        name="exchange",
    )(seg, segcol, order, query, pairs, student_rows, projection)


def local(query, key, value, segment_ids, student_rows, projection, send_order):
    rows = query.shape[0]
    n = lax.axis_size("seq")
    cols = COLS
    bands = n // cols
    width = HQ * HD // cols
    depth = projection.shape[0]
    ds = student_rows.shape[1]
    share = rows // n
    near = [[b * cols + c for c in range(cols)] for b in range(bands)]

    pairs = jnp.concatenate([key, value], axis=1)
    band_rows, column, arrived = exchange(
        query, pairs, segment_ids, student_rows, projection, send_order
    )
    band_rows = band_rows.reshape(cols * rows, ds)
    column = column.reshape(n * depth, width)
    target = arrived.reshape(n, cols, share, width).transpose(1, 0, 2, 3).reshape(cols * rows, width)
    predicted = jnp.dot(band_rows, column, preferred_element_type=jnp.float32)
    residual = (predicted - target.astype(jnp.float32)).astype(jnp.bfloat16)
    proj_part = lax.dot_general(
        band_rows, residual, (((0,), (0,)), ((), ())), preferred_element_type=jnp.float32
    ).astype(jnp.bfloat16)
    proj_parts = lax.all_to_all(
        proj_part.reshape(n, depth, width), "seq", split_axis=0, concat_axis=0, tiled=True
    )
    rows_part = lax.dot_general(
        residual, column, (((1,), (1,)), ((), ())), preferred_element_type=jnp.float32
    ).astype(jnp.bfloat16)
    rows_parts = lax.all_to_all(
        rows_part.reshape(cols, rows, ds),
        "seq", split_axis=0, concat_axis=0, tiled=True, axis_index_groups=near,
    )
    grad_rows = jnp.sum(rows_parts.astype(jnp.float32), axis=0).astype(jnp.bfloat16)
    grad_scale = (rows * n) ** (-0.5)
    summed = jnp.sum(proj_parts.reshape(bands, cols, depth, width).astype(jnp.float32), axis=0)
    grad_proj = (summed * grad_scale).transpose(1, 0, 2).reshape(depth, cols * width)
    return (grad_rows, grad_proj)


def solution(mesh):
    both = ("groups", "seq")
    return jax.shard_map(
        local,
        mesh=mesh,
        in_specs=(
            P(both, None), P(both, None), P(both, None), P(both), P(both, None),
            P("seq", None), P(both, None),
        ),
        out_specs=(P(both, None), P(both, None)),
        check_vma=False,
    )
```

time: 219 us -> 199 us (0.909)
  Pallas kernels: 0 us -> 89.6 us
  blocking collectives: 75.5 us -> 0 us
  between operations: 14.4 us -> 0.73 us
  matrix products: 21.9 us -> 12.1 us
  starting transfers between devices: 14.9 us -> 7.53 us
  waiting for transfers between devices: 69.8 us -> 67.2 us
    pallas_call x0 -> x1, Pallas kernels: none -> 89.6 us  [exchange(): pl.pallas_call(functools.partial(reach_kernel, n), out_shape=(jax.ShapeDt...]
    all_to_all x2 -> x0, blocking collectives: 75.5 us -> none  [the longest x1 62.1 us: local(): lax.all_to_all(outgoing.reshape(n, cols * share, width), 'seq', split_axi...]
    ppermute x3 -> x0, starting transfers between devices: 7.75 us -> none  [shifted(): lax.ppermute(value, axis, [(s, s + steps) for s in range(count - steps)])]
    dot_general x4 -> x0, matrix products: 4.16 us -> none  [attention(): jnp.einsum('hqk,kd->qhd', weights, v, preferred_element_type=jnp.float32)]
    ppermute x3 -> x0, waiting for transfers between devices: 4.13 us -> none  [shifted(): lax.ppermute(value, axis, [(s, s + steps) for s in range(count - steps)])]
    all_to_all x1, waiting for transfers between devices: 29 us -> 32.7 us  [local(): lax.all_to_all(rows_part.reshape(cols, rows, ds), 'seq', split_axis=0, co...]
    sub x4 -> x0, matrix products: 3.07 us -> none  [attention(): weights = jnp.exp(scores - top)]
    convert_element_type x3, local copies, waits for them, and re-layouts: 5.31 us -> 8.37 us  [local(): residual = (predicted - target.astype(jnp.float32)).astype(jnp.bfloat16)]
  transfers between devices with their start and end apart: 7 -> 2, of which waited for: 4 -> 2; matrix products, arithmetic and copies ran while one was open for 14% -> 4% of each run, Pallas kernels for 0% -> 0%
where the time goes in v2:
time: 199 us; the launch traced here: 198 us
  Pallas kernels  89.6 us (45%)
  waiting for transfers between devices  67.2 us (34%)
  local copies, waits for them, and re-layouts  16.3 us (8%)
  matrix products  12.1 us (6%)
  starting transfers between devices  7.53 us (4%)
  other arithmetic  4.5 us (2%)
    pallas_call x1, Pallas kernels, exchange(): pl.pallas_call(functools.partial(reach_kernel, n), out_shape=(jax.ShapeDt...  89.6 us
    all_to_all x1, waiting for transfers between devices, local(): lax.all_to_all(proj_part.reshape(n, depth, width), 'seq', split_axis=0, c...  34.6 us
    all_to_all x1, waiting for transfers between devices, local(): lax.all_to_all(rows_part.reshape(cols, rows, ds), 'seq', split_axis=0, co...  32.7 us
    convert_element_type x3, local copies, waits for them, and re-layouts, local(): residual = (predicted - target.astype(jnp.float32)).astype(jnp.bfloat16)  8.37 us
    dot_general x1, matrix products, local(): lax.dot_general(band_rows, residual, (((0,), (0,)), ((), ())), preferred_...  5.22 us
    unnamed x18, local copies, waits for them, and re-layouts  4.87 us
    all_to_all x1, starting transfers between devices, local(): lax.all_to_all(rows_part.reshape(cols, rows, ds), 'seq', split_axis=0, co...  4.44 us
  transfers between devices with their start and end apart: 2, of which 2 were waited for; matrix products, arithmetic and copies ran while one was open for 4% of the time, Pallas kernels for 0%

profile of v2, /device:TPU:0, one launch (start us, length us, event | category | flops | bytes accessed | tf_op | source)
XLA Modules:
  0.0 198.0 jit_solution(8843911999432102015)
XLA Ops:
  0.6 1.0 pad_maximum_fusion.pairs_ref
  1.6 0.7 broadcast_in_dim.8.seg_ref
  2.3 0.7 broadcast_in_dim.22.order_ref
  3.0 0.7 broadcast_in_dim.9.segcol_ref
  3.8 0.0 copy-start
  3.8 1.2 copy-done
  5.0 0.0 copy-start.1
  5.0 1.0 copy-done.1
  6.0 0.0 copy-start.2
  6.0 1.0 copy-done.2
  7.0 89.6 %exchange.1 = (bf16[8,128,1536]{2,1,0:T(8,128)(2,1)S(1)}, bf16[32,48,512]{2,1,0:T(8,128)(2,1)S(1)}, bf16[32,32,512]{2,1,0:T(8,128)(2,1)S(1)}) custom-call(s32[8,128]{1,0:T(8,128)S(1)} %broadcast_in_dim.8.seg_ref, s32[128,128]{1,0:T(8,128)S(1)} %broadcast_in_dim.9.segcol_ref, s32[128,128]{1,0:T(8,128)S(1)} %broadcast_in_dim.22.order_ref, ...), custom_call_target="tpu_custom_call" | custom-call | tf_op jit(solution)/shard_map/exchange/pallas_call | solution.py:152
  96.6 0.0 copy-start.3
  96.6 1.6 copy-done.3
  98.3 0.0 copy-start.5
  98.3 1.9 reshape.38
  100.1 0.0 copy-done.5
  100.1 3.4 %copy.11 = f32[8,32,4,512]{3,2,1,0:T(4,128)} copy(f32[8,32,4,512]{3,2,0,1:T(4,128)} %bitcast.20) | data formatting | bytes 4194304 | tf_op jit(solution)/shard_map/convert_element_type | solution.py:193
  103.5 0.0 copy-start.4
  103.5 3.1 %reshape.36 = f32[1024,512]{1,0:T(8,128)} reshape(f32[8,32,4,512]{3,2,1,0:T(4,128)} %copy.11) | data formatting | bytes 4194304 | tf_op jit(solution)/shard_map/convert_element_type | solution.py:193
  106.6 0.0 copy-done.4
  106.6 0.0 copy-start.6
  106.6 0.0 copy-start.7
  106.7 3.3 %fusion = f32[1024,512]{1,0:T(8,128)S(1)} fusion(bf16[1024,1536]{1,0:T(8,128)(2,1)S(1)} %bitcast.16, bf16[1536,512]{1,0:T(8,128)(2,1)} %bitcast.18), kind=kOutput, calls=%fused_computation.6 | convolution fusion | flops 1610612736 | bytes 6815744 | tf_op jit(solution)/shard_map/dot_general | solution.py:192
  110.0 0.0 copy-done.6
  110.0 0.0 copy-done.7
  110.0 0.0 copy-start.8
  110.0 3.5 %convolution_convert_fusion = bf16[1024,1536]{1,0:T(8,128)(2,1)} fusion(bf16[1536,512]{1,0:T(8,128)(2,1)S(1)} %bitcast.19, f32[1024,512]{1,0:T(8,128)S(1)} %fusion, f32[1024,512]{1,0:T(8,128)S(1)} %copy-done.7), kind=kOutput, calls=%fused_computation | convolution fusion | flops 1613234176 | bytes 8912896 | tf_op jit(solution)/shard_map/dot_general | solution.py:200
  113.6 0.0 copy-done.8
  113.6 4.4 %all-to-all-start = ((bf16[8,128,1536]{2,1,0:T(8,128)(2,1)}), bf16[8,128,1536]{2,1,0:T(8,128)(2,1)}, u32[]{:S(2)}, u32[]{:S(2)}) async-start(bf16[8,128,1536]{2,1,0:T(8,128)(2,1)} %bitcast.22), calls=%async_computation | async-start | bytes 6291456 | tf_op jit(solution)/shard_map/all_to_all | solution.py:203
  118.0 5.2 %convolution_convert_fusion.1 = bf16[1536,512]{1,0:T(8,128)(2,1)} fusion(bf16[1024,1536]{1,0:T(8,128)(2,1)S(1)} %bitcast.17, f32[1024,512]{1,0:T(8,128)} %copy-done.8, f32[1024,512]{1,0:T(8,128)} %reshape.36), kind=kOutput, calls=%fused_computation.2 | convolution fusion | flops 1612447744 | bytes 8912896 | tf_op jit(solution)/shard_map/dot_general | solution.py:194
  123.2 32.7 %all-to-all-done = bf16[8,128,1536]{2,1,0:T(8,128)(2,1)} async-done(((bf16[8,128,1536]{2,1,0:T(8,128)(2,1)}), bf16[8,128,1536]{2,1,0:T(8,128)(2,1)}, u32[]{:S(2)}, u32[]{:S(2)}) %all-to-all-start) | async-done | bytes 3145760 | tf_op jit(solution)/shard_map/all_to_all | solution.py:203
  155.9 3.1 %all-to-all-start.1 = ((bf16[32,48,512]{2,1,0:T(8,128)(2,1)}), bf16[32,48,512]{2,1,0:T(8,128)(2,1)S(1)}, u32[]{:S(2)}, u32[]{:S(2)}) async-start(bf16[32,48,512]{2,1,0:T(8,128)(2,1)} %bitcast.23), calls=%async_computation.1 | async-start | bytes 3145728 | tf_op jit(solution)/shard_map/all_to_all | solution.py:197
  159.0 3.2 %reduce_sum.21 = bf16[128,1536]{1,0:T(8,128)(2,1)} reduce(bf16[8,128,1536]{2,1,0:T(8,128)(2,1)} %all-to-all-done, bf16[]{:T(256)} %constant.1.clone.1), dimensions={0}, to_apply=%region_0.0 | reduce | flops 1376256 | bytes 3538946 | tf_op jit(solution)/shard_map/reduce_sum | solution.py:207
  162.2 34.6 %all-to-all-done.1 = bf16[32,48,512]{2,1,0:T(8,128)(2,1)S(1)} async-done(((bf16[32,48,512]{2,1,0:T(8,128)(2,1)}), bf16[32,48,512]{2,1,0:T(8,128)(2,1)S(1)}, u32[]{:S(2)}, u32[]{:S(2)}) %all-to-all-start.1) | async-done | bytes 1572896 | tf_op jit(solution)/shard_map/all_to_all | solution.py:197
  196.7 0.2 convert_reduce_fusion
  197.0 0.1 multiply_bitcast_fusion
  197.1 0.9 copy.13
Async XLA Ops:
  3.8 1.2 copy-start
  5.0 1.0 copy-start.1
  6.0 1.0 copy-start.2
  96.6 1.6 copy-start.3
  98.3 1.9 copy-start.5
  103.5 3.1 %copy-start.4 = (bf16[8,128,1536]{2,1,0:T(8,128)(2,1)S(1)}, bf16[8,128,1536]{2,1,0:T(8,128)(2,1)}, u32[]{:S(2)}) copy-start(bf16[8,128,1536]{2,1,0:T(8,128)(2,1)} %copy-done.3) | copy-start | bytes 9437188
  106.6 3.4 %copy-start.6 = (bf16[32,48,512]{2,1,0:T(8,128)(2,1)S(1)}, bf16[32,48,512]{2,1,0:T(8,128)(2,1)}, u32[]{:S(2)}) copy-start(bf16[32,48,512]{2,1,0:T(8,128)(2,1)} %copy-done.5) | copy-start | bytes 4718596
  106.6 3.4 %copy-start.7 = (f32[1024,512]{1,0:T(8,128)S(1)}, f32[1024,512]{1,0:T(8,128)}, u32[]{:S(2)}) copy-start(f32[1024,512]{1,0:T(8,128)} %reshape.36) | copy-start | bytes 6291460
  110.0 3.6 %copy-start.8 = (f32[1024,512]{1,0:T(8,128)}, f32[1024,512]{1,0:T(8,128)S(1)}, u32[]{:S(2)}) copy-start(f32[1024,512]{1,0:T(8,128)S(1)} %fusion) | copy-start | bytes 6291460
  113.6 42.3 %all-to-all-start = ((bf16[8,128,1536]{2,1,0:T(8,128)(2,1)}), bf16[8,128,1536]{2,1,0:T(8,128)(2,1)}, u32[]{:S(2)}, u32[]{:S(2)}) async-start(bf16[8,128,1536]{2,1,0:T(8,128)(2,1)} %bitcast.22), calls=%async_computation | async-start | bytes 6291456 | tf_op jit(solution)/shard_map/all_to_all | solution.py:203
  155.9 40.8 %all-to-all-start.1 = ((bf16[32,48,512]{2,1,0:T(8,128)(2,1)}), bf16[32,48,512]{2,1,0:T(8,128)(2,1)S(1)}, u32[]{:S(2)}, u32[]{:S(2)}) async-start(bf16[32,48,512]{2,1,0:T(8,128)(2,1)} %bitcast.23), calls=%async_computation.1 | async-start | bytes 3145728 | tf_op jit(solution)/shard_map/all_to_all | solution.py:197

commit v3 on v2

--- a/solution.py
+++ b/solution.py
@@ -42,8 +42,19 @@
         block = proj_ref.at[:, pl.ds(pl.multiple_of((peer % cols) * width, width), width)]
         return remote(block, column_ref.at[place], col_send.at[slot], col_recv.at[place], peer)
 
-    def row_copy(peer, slot, place):
-        return remote(rows_ref, band_ref.at[place], row_send.at[slot], row_recv.at[place], peer)
+    parity, chip, chips = my_col % 2, my_col // 2, cols // 2
+    twin = me + 1 - 2 * parity
+
+    def row_copy(k, place):
+        peer = my_band * cols + 2 * ((chip + k) % chips) + parity
+        return remote(rows_ref, band_ref.at[place], row_send.at[k], row_recv.at[place], peer)
+
+    def twin_copy(place):
+        return remote(rows_ref, band_ref.at[place], row_send.at[0], row_recv.at[place], twin)
+
+    def pass_copy(k, source, place):
+        return remote(band_ref.at[source], band_ref.at[place], row_send.at[chips + k],
+                      row_recv.at[place], twin)
 
     def out_copy(peer, place):
         return remote(outgoing.at[peer % cols, peer // cols], arrived_ref.at[place],
@@ -70,9 +81,9 @@
     own[0].start()
     own[1].start()
 
-    @pl.loop(1, cols)
-    def _(k):
-        row_copy(my_band * cols + (my_col + k) % cols, k, my_col).start()
+    for k in range(1, cols // 2):
+        row_copy(k, my_col).start()
+    twin_copy(my_col).start()
 
     @pl.loop(1, n)
     def _(k):
@@ -123,12 +134,16 @@
                 out_copy(peer, me).start()
 
     own[2].start()
+    for k in range(1, cols // 2):
+        place = 2 * ((chip + chips - k) % chips) + parity
+        row_copy(k, place).wait()
+        pass_copy(k, place, place).start()
     for copy in own:
         copy.wait()
-
-    @pl.loop(1, cols)
-    def _(k):
-        row_copy(my_band * cols + (my_col + k) % cols, k, (my_col + cols - k) % cols).wait()
+    twin_copy(2 * chip + 1 - parity).wait()
+    for k in range(1, cols // 2):
+        place = 2 * ((chip + chips - k) % chips)
+        pass_copy(k, place + parity, place + 1 - parity).wait()
 
     @pl.loop(1, n)
     def _(k):
@@ -171,6 +186,111 @@
     )(seg, segcol, order, query, pairs, student_rows, projection)
 
 
+def share_kernel(n, scale, resid_ref, column_ref, part_ref, grows_ref, gproj_ref,
+                 twin_out, twin_in, rows_out, rows_in, proj_in,
+                 twin_send, twin_recv, row_send, row_recv, proj_send, proj_recv, own_sem):
+    me = lax.axis_index("seq")
+    cols = COLS
+    bands = n // cols
+    band, col = me // cols, me % cols
+    parity, chip, chips = col % 2, col // 2, cols // 2
+    twin = me + 1 - 2 * parity
+    rows = grows_ref.shape[0]
+    width = resid_ref.shape[1]
+
+    def remote(src, dst, send, recv, peer):
+        return pltpu.make_async_remote_copy(
+            src_ref=src, dst_ref=dst, send_sem=send, recv_sem=recv,
+            device_id={"seq": peer}, device_id_type=MESH)
+
+    def proj_copy(k, place):
+        peer = (me + k) % n
+        return remote(part_ref.at[peer], proj_in.at[place], proj_send.at[k], proj_recv.at[place], peer)
+
+    def twin_copy(t):
+        return remote(twin_out.at[t], twin_in.at[t], twin_send.at[t], twin_recv.at[t], twin)
+
+    def row_copy(k, place):
+        t = (chip + k) % chips
+        return remote(rows_out.at[k], rows_in.at[place], row_send.at[k], row_recv.at[place],
+                      band * cols + 2 * t + parity)
+
+    def product(j):
+        block = resid_ref[pl.ds(pl.multiple_of(j * rows, rows), rows), :]
+        return lax.dot_general(
+            block, column_ref[...], (((1,), (1,)), ((), ())), preferred_element_type=jnp.float32)
+
+    barrier = pltpu.get_barrier_semaphore()
+
+    @pl.loop(1, n)
+    def _(k):
+        pl.semaphore_signal(barrier, inc=1, device_id={"seq": (me + k) % n}, device_id_type=MESH)
+
+    pl.semaphore_wait(barrier, n - 1)
+
+    @pl.loop(1, n)
+    def _(k):
+        proj_copy(k, me).start()
+
+    own = pltpu.make_async_copy(part_ref.at[me], proj_in.at[me], own_sem.at[0])
+    own.start()
+    for k in range(1, cols // 2 + 1):
+        t = (chip + k) % chips
+        twin_out[t] = product(2 * t + 1 - parity).astype(jnp.bfloat16)
+        twin_copy(t).start()
+    for k in range(1, cols // 2 + 1):
+        t = (chip + k) % chips
+        part = product(2 * t + parity)
+        twin_copy(t).wait()
+        part = part + twin_in[t].astype(jnp.float32)
+        if k < cols // 2:
+            rows_out[k] = part.astype(jnp.bfloat16)
+            row_copy(k, chip).start()
+    for k in range(1, cols // 2):
+        place = (chip + chips - k) % chips
+        row_copy(k, place).wait()
+        part = part + rows_in[place].astype(jnp.float32)
+    grows_ref[...] = part.astype(jnp.bfloat16)
+    own.wait()
+
+    @pl.loop(1, n)
+    def _(k):
+        proj_copy(k, (me + n - k) % n).wait()
+
+    @pl.loop(0, cols)
+    def _(c):
+        def add(b, total):
+            return total + proj_in[b * cols + c].astype(jnp.float32)
+
+        total = lax.fori_loop(1, bands, add, proj_in[c].astype(jnp.float32))
+        gproj_ref[:, pl.ds(pl.multiple_of(c * width, width), width)] = total * scale
+
+
+def share(residual, column, parts, rows, scale):
+    n, depth, width = parts.shape
+    ds = column.shape[0]
+    vmem = pl.BlockSpec(memory_space=pltpu.VMEM)
+    dma = pltpu.SemaphoreType.DMA
+    bf16 = jnp.bfloat16
+    half = COLS // 2
+    return pl.pallas_call(
+        functools.partial(share_kernel, n, scale),
+        out_shape=(
+            jax.ShapeDtypeStruct((rows, ds), bf16),
+            jax.ShapeDtypeStruct((depth, COLS * width), jnp.float32),
+        ),
+        in_specs=[vmem] * 2 + [pl.BlockSpec(memory_space=pl.ANY)],
+        out_specs=(vmem, vmem),
+        scratch_shapes=[pltpu.VMEM((half, rows, ds), bf16)] * 4 + [
+            pltpu.VMEM((n, depth, width), bf16),
+            dma((half,)), dma((half,)), dma((half,)), dma((half,)), dma((n,)), dma((n,)), dma((1,)),
+        ],
+        compiler_params=pltpu.CompilerParams(
+            collective_id=1, has_side_effects=True, vmem_limit_bytes=40 * 1024 * 1024),
+        name="share",
+    )(residual, column, parts)
+
+
 def local(query, key, value, segment_ids, student_rows, projection, send_order):
     rows = query.shape[0]
     n = lax.axis_size("seq")
@@ -179,35 +299,23 @@
     width = HQ * HD // cols
     depth = projection.shape[0]
     ds = student_rows.shape[1]
-    share = rows // n
-    near = [[b * cols + c for c in range(cols)] for b in range(bands)]
-
+    each = rows // n
     pairs = jnp.concatenate([key, value], axis=1)
     band_rows, column, arrived = exchange(
         query, pairs, segment_ids, student_rows, projection, send_order
     )
     band_rows = band_rows.reshape(cols * rows, ds)
     column = column.reshape(n * depth, width)
-    target = arrived.reshape(n, cols, share, width).transpose(1, 0, 2, 3).reshape(cols * rows, width)
+    target = arrived.reshape(n, cols, each, width).transpose(1, 0, 2, 3).reshape(cols * rows, width)
     predicted = jnp.dot(band_rows, column, preferred_element_type=jnp.float32)
     residual = (predicted - target.astype(jnp.float32)).astype(jnp.bfloat16)
     proj_part = lax.dot_general(
         band_rows, residual, (((0,), (0,)), ((), ())), preferred_element_type=jnp.float32
     ).astype(jnp.bfloat16)
-    proj_parts = lax.all_to_all(
-        proj_part.reshape(n, depth, width), "seq", split_axis=0, concat_axis=0, tiled=True
+    grad_scale = (rows * n) ** (-0.5)
+    grad_rows, grad_proj = share(
+        residual, column, proj_part.reshape(n, depth, width), rows, grad_scale
     )
-    rows_part = lax.dot_general(
-        residual, column, (((1,), (1,)), ((), ())), preferred_element_type=jnp.float32
-    ).astype(jnp.bfloat16)
-    rows_parts = lax.all_to_all(
-        rows_part.reshape(cols, rows, ds),
-        "seq", split_axis=0, concat_axis=0, tiled=True, axis_index_groups=near,
-    )
-    grad_rows = jnp.sum(rows_parts.astype(jnp.float32), axis=0).astype(jnp.bfloat16)
-    grad_scale = (rows * n) ** (-0.5)
-    summed = jnp.sum(proj_parts.reshape(bands, cols, depth, width).astype(jnp.float32), axis=0)
-    grad_proj = (summed * grad_scale).transpose(1, 0, 2).reshape(depth, cols * width)
     return (grad_rows, grad_proj)
 
 

time: 199 us -> 154 us (0.77)
  waiting for transfers between devices: 67.2 us -> 0 us
  Pallas kernels: 89.6 us -> 129 us
  starting transfers between devices: 7.53 us -> 0 us
  matrix products: 12.1 us -> 6.29 us
  other arithmetic: 4.5 us -> 1 us
    all_to_all x2 -> x0, waiting for transfers between devices: 67.2 us -> none  [the longest x1 34.6 us: local(): lax.all_to_all(proj_part.reshape(n, depth, width), 'seq', split_axis=0, c...]
    pallas_call x0 -> x1, Pallas kernels: none -> 51.6 us  [share(): pl.pallas_call(functools.partial(share_kernel, n, scale), out_shape=(jax....]
    pallas_call x1, Pallas kernels: 89.6 us -> 77.7 us  [exchange(): pl.pallas_call(functools.partial(reach_kernel, n), out_shape=(jax.ShapeDt...]
    all_to_all x2 -> x0, starting transfers between devices: 7.53 us -> none  [the longest x1 4.44 us: local(): lax.all_to_all(rows_part.reshape(cols, rows, ds), 'seq', split_axis=0, co...]
    dot_general x1 -> x0, matrix products: 3.54 us -> none  [local(): lax.dot_general(residual, column, (((1,), (1,)), ((), ())), preferred_ele...]
    reduce_sum x2 -> x0, other arithmetic: 3.42 us -> none  [the longest x1 3.18 us: local(): jnp.sum(rows_parts.astype(jnp.float32), axis=0).astype(jnp.bfloat16)]
    dot_general x1, matrix products: 5.22 us -> 1.83 us  [local(): lax.dot_general(band_rows, residual, (((0,), (0,)), ((), ())), preferred_...]
    unnamed x18 -> x12, local copies, waits for them, and re-layouts: 4.87 us -> 6.48 us
  transfers between devices with their start and end apart: 2 -> 0, of which waited for: 2 -> 0; matrix products, arithmetic and copies ran while one was open for 4% -> 0% of each run, Pallas kernels for 0% -> 0%
where the time goes in v3:
time: 154 us
  Pallas kernels  129 us (84%)
  local copies, waits for them, and re-layouts  16.6 us (11%)
  matrix products  6.29 us (4%)
    pallas_call x1, Pallas kernels, exchange(): pl.pallas_call(functools.partial(reach_kernel, n), out_shape=(jax.ShapeDt...  77.7 us
    pallas_call x1, Pallas kernels, share(): pl.pallas_call(functools.partial(share_kernel, n, scale), out_shape=(jax....  51.6 us
    convert_element_type x3, local copies, waits for them, and re-layouts, local(): residual = (predicted - target.astype(jnp.float32)).astype(jnp.bfloat16)  8.02 us
    unnamed x12, local copies, waits for them, and re-layouts  6.48 us
    dot_general x1, matrix products, local(): predicted = jnp.dot(band_rows, column, preferred_element_type=jnp.float32)  4.46 us

profile of v3, /device:TPU:0, one launch (start us, length us, event | category | flops | bytes accessed | tf_op | source)
XLA Modules:
  0.0 153.9 jit_solution(18240723592606158311)
XLA Ops:
  0.6 0.7 broadcast_in_dim.8.seg_ref
  1.3 0.7 broadcast_in_dim.22.order_ref
  2.0 0.7 broadcast_in_dim.9.segcol_ref
  2.8 1.0 pad_maximum_fusion.pairs_ref
  3.8 0.0 copy-start
  3.8 1.2 copy-done
  5.0 0.0 copy-start.1
  5.0 1.0 copy-done.1
  6.0 0.0 copy-start.2
  6.0 1.0 copy-done.2
  7.0 77.7 %exchange.1 = (bf16[8,128,1536]{2,1,0:T(8,128)(2,1)S(1)}, bf16[32,48,512]{2,1,0:T(8,128)(2,1)S(1)}, bf16[32,32,512]{2,1,0:T(8,128)(2,1)S(1)}) custom-call(s32[8,128]{1,0:T(8,128)S(1)} %broadcast_in_dim.8.seg_ref, s32[128,128]{1,0:T(8,128)S(1)} %broadcast_in_dim.9.segcol_ref, s32[128,128]{1,0:T(8,128)S(1)} %broadcast_in_dim.22.order_ref, ...), custom_call_target="tpu_custom_call" | custom-call | tf_op jit(solution)/shard_map/exchange/pallas_call | solution.py:167
  84.7 0.0 copy-start.3
  84.7 1.6 %copy-done.3 = bf16[8,128,1536]{2,1,0:T(8,128)(2,1)} copy-done((bf16[8,128,1536]{2,1,0:T(8,128)(2,1)}, bf16[8,128,1536]{2,1,0:T(8,128)(2,1)S(1)}, u32[]{:S(2)}) %copy-start.3) | copy-done | bytes 3145752
  86.4 1.7 %reshape.26 = f32[32,8,4,512]{3,2,1,0:T(4,128)} reshape(bf16[32,32,512]{2,1,0:T(8,128)(2,1)S(1)} %get-tuple-element.7) | data formatting | bytes 3145728 | tf_op jit(solution)/shard_map/convert_element_type | solution.py:311
  88.0 3.4 %copy.11 = f32[32,8,4,512]{3,2,0,1:T(4,128)} copy(f32[32,8,4,512]{3,2,1,0:T(4,128)} %reshape.26) | data formatting | bytes 4194304 | tf_op jit(solution)/shard_map/convert_element_type | solution.py:311
  91.4 3.0 %reshape.25 = f32[1024,512]{1,0:T(8,128)} reshape(f32[8,32,4,512]{3,2,1,0:T(4,128)} %bitcast.16) | data formatting | bytes 4194304 | tf_op jit(solution)/shard_map/convert_element_type | solution.py:311
  94.4 0.0 copy-start.4
  94.4 4.5 %subtract_convert_fusion.resid_ref = bf16[1024,512]{1,0:T(8,128)(2,1)S(1)} fusion(f32[1024,512]{1,0:T(8,128)} %reshape.25, bf16[1024,1536]{1,0:T(8,128)(2,1)} %bitcast.14, bf16[1536,512]{1,0:T(8,128)(2,1)S(1)} %bitcast.11), kind=kOutput, calls=%fused_computation.2 | convolution fusion | flops 1611661312 | bytes 7864320 | tf_op jit(solution)/shard_map/dot_general | solution.py:310
  98.8 0.0 copy-done.4
  98.9 1.8 %convolution_convert_fusion = bf16[1536,512]{1,0:T(8,128)(2,1)S(1)} fusion(bf16[1024,1536]{1,0:T(8,128)(2,1)S(1)} %bitcast.15, bf16[1024,512]{1,0:T(8,128)(2,1)S(1)} %subtract_convert_fusion.resid_ref), kind=kOutput, calls=%fused_computation | convolution fusion | flops 1611399168 | bytes 5767168 | tf_op jit(solution)/shard_map/dot_general | solution.py:312
  100.7 51.6 %share.1 = (bf16[128,1536]{1,0:T(8,128)(2,1)S(1)}, f32[48,4096]{1,0:T(8,128)S(1)}) custom-call(bf16[1024,512]{1,0:T(8,128)(2,1)S(1)} %subtract_convert_fusion.resid_ref, bf16[1536,512]{1,0:T(8,128)(2,1)S(1)} %bitcast.12, bf16[32,48,512]{2,1,0:T(8,128)(2,1)S(1)} %bitcast.13), custom_call_target="tpu_custom_call" | custom-call | tf_op jit(solution)/shard_map/share/pallas_call | solution.py:276
  152.3 0.7 copy.14
  153.0 0.9 copy.15
Async XLA Ops:
  3.8 1.2 copy-start
  5.0 1.0 copy-start.1
  6.0 1.0 copy-start.2
  84.7 1.7 %copy-start.3 = (bf16[8,128,1536]{2,1,0:T(8,128)(2,1)}, bf16[8,128,1536]{2,1,0:T(8,128)(2,1)S(1)}, u32[]{:S(2)}) copy-start(bf16[8,128,1536]{2,1,0:T(8,128)(2,1)S(1)} %get-tuple-element.5) | copy-start | bytes 9437188
  94.4 4.5 %copy-start.4 = (bf16[8,128,1536]{2,1,0:T(8,128)(2,1)S(1)}, bf16[8,128,1536]{2,1,0:T(8,128)(2,1)}, u32[]{:S(2)}) copy-start(bf16[8,128,1536]{2,1,0:T(8,128)(2,1)} %copy-done.3) | copy-start | bytes 9437188

commit v4 on v3

--- a/solution.py
+++ b/solution.py
@@ -18,7 +18,7 @@
 def reach_kernel(n, seg_ref, segcol_ref, order_ref, query_ref, pairs_ref, rows_ref, proj_ref,
                  band_ref, column_ref, arrived_ref, pairs_in, ids_in, outgoing,
                  pair_send, pair_recv, id_send, id_recv, col_send, col_recv,
-                 row_send, row_recv, out_send, out_recv, own_sem):
+                 row_send, row_recv, out_send, out_recv, own_sem, hop_send, hop_recv):
     me = lax.axis_index("seq")
     cols = COLS
     bands = n // cols
@@ -68,6 +68,35 @@
         pltpu.make_async_copy(outgoing.at[my_col, my_band], arrived_ref.at[me], own_sem.at[2]),
     ]
 
+    def hop(b, way):
+        slab = column_ref.at[pl.ds(b * cols, cols)]
+        peer = (me + n + (cols if way == 0 else -cols)) % n
+        return remote(slab, slab, hop_send.at[way, b], hop_recv.at[b], peer)
+
+    def up(i):
+        return (my_band - i >= 0) & (my_band + 1 < bands)
+
+    def down(i):
+        return (my_band + i < bands) & (my_band - 1 >= 0)
+
+    def hops(i, first=False):
+        if not first:
+            @pl.when(my_band - i >= 0)
+            def _():
+                hop(my_band - i, 0).wait_recv()
+
+            @pl.when(my_band + i < bands)
+            def _():
+                hop(my_band + i, 1).wait_recv()
+
+        @pl.when(up(i))
+        def _():
+            hop(my_band - i, 0).start()
+
+        @pl.when(down(i))
+        def _():
+            hop(my_band + i, 1).start()
+
     barrier = pltpu.get_barrier_semaphore()
 
     @pl.loop(1, n)
@@ -75,20 +104,30 @@
         pl.semaphore_signal(barrier, inc=1, device_id={"seq": (me + k) % n}, device_id_type=MESH)
 
     pl.semaphore_wait(barrier, n - 1)
+    own[1].start()
+
+    @pl.loop(1, cols)
+    def _(k):
+        col_copy(my_band * cols + (my_col + k) % cols, k, me).start()
+
     for k in range(1, REACH + 1):
         id_copy(k).start()
         pair_copy(k).start()
     own[0].start()
-    own[1].start()
 
     for k in range(1, cols // 2):
         row_copy(k, my_col).start()
     twin_copy(my_col).start()
 
-    @pl.loop(1, n)
-    def _(k):
-        col_copy((me + k) % n, k, me).start()
-
+
+    own[1].wait()
+
+    @pl.loop(1, cols)
+    def _(k):
+        col_copy(my_band * cols + (my_col + k) % cols, k,
+                 my_band * cols + (my_col + cols - k) % cols).wait()
+
+    hops(0, True)
     for k in range(1, REACH + 1):
         id_copy(k).wait()
         pair_copy(k).wait()
@@ -133,13 +172,33 @@
             def _():
                 out_copy(peer, me).start()
 
+        @pl.when(c == cols // 2)
+        def _():
+            hops(1)
+
     own[2].start()
+
+    @pl.loop(2, bands)
+    def _(i):
+        hops(i)
+
     for k in range(1, cols // 2):
         place = 2 * ((chip + chips - k) % chips) + parity
         row_copy(k, place).wait()
         pass_copy(k, place, place).start()
-    for copy in own:
-        copy.wait()
+    own[0].wait()
+    own[2].wait()
+
+    @pl.loop(0, bands)
+    def _(i):
+        @pl.when(up(i))
+        def _():
+            hop(my_band - i, 0).wait_send()
+
+        @pl.when(down(i))
+        def _():
+            hop(my_band + i, 1).wait_send()
+
     twin_copy(2 * chip + 1 - parity).wait()
     for k in range(1, cols // 2):
         place = 2 * ((chip + chips - k) % chips)
@@ -147,7 +206,6 @@
 
     @pl.loop(1, n)
     def _(k):
-        col_copy((me + k) % n, k, (me + n - k) % n).wait()
         out_copy((me + k) % n, (me + n - k) % n).wait()
 
 
@@ -179,6 +237,7 @@
             pltpu.VMEM((COLS, bands, rows // bands, width), bf16),
             dma((REACH,)), dma((REACH,)), dma((REACH,)), dma((REACH,)),
             dma((n,)), dma((n,)), dma((COLS,)), dma((COLS,)), dma((n,)), dma((n,)), dma((3,)),
+            dma((2, bands)), dma((bands,)),
         ],
         compiler_params=pltpu.CompilerParams(
             collective_id=0, has_side_effects=True, vmem_limit_bytes=40 * 1024 * 1024),

time: 154 us -> 148 us (0.961)
  Pallas kernels: 129 us -> 123 us
    pallas_call x1, Pallas kernels: 51.6 us -> 45.1 us  [share(): pl.pallas_call(functools.partial(share_kernel, n, scale), out_shape=(jax....]
where the time goes in v4:
time: 148 us
  Pallas kernels  123 us (83%)
  local copies, waits for them, and re-layouts  16.6 us (11%)
  matrix products  6.31 us (4%)
    pallas_call x1, Pallas kernels, exchange(): pl.pallas_call(functools.partial(reach_kernel, n), out_shape=(jax.ShapeDt...  78.3 us
    pallas_call x1, Pallas kernels, share(): pl.pallas_call(functools.partial(share_kernel, n, scale), out_shape=(jax....  45.1 us
    convert_element_type x3, local copies, waits for them, and re-layouts, local(): residual = (predicted - target.astype(jnp.float32)).astype(jnp.bfloat16)  8.02 us
    unnamed x12, local copies, waits for them, and re-layouts  6.48 us
    dot_general x1, matrix products, local(): predicted = jnp.dot(band_rows, column, preferred_element_type=jnp.float32)  4.47 us

profile of v4, /device:TPU:0, one launch (start us, length us, event | category | flops | bytes accessed | tf_op | source)
XLA Modules:
  0.0 148.0 jit_solution(10372981018978461571)
XLA Ops:
  0.6 0.7 broadcast_in_dim.8.seg_ref
  1.3 0.7 broadcast_in_dim.22.order_ref
  2.0 0.7 broadcast_in_dim.9.segcol_ref
  2.8 1.0 pad_maximum_fusion.pairs_ref
  3.8 0.0 copy-start
  3.8 1.2 copy-done
  5.0 0.0 copy-start.1
  5.0 1.0 copy-done.1
  6.0 0.0 copy-start.2
  6.0 1.0 copy-done.2
  7.0 78.3 %exchange.1 = (bf16[8,128,1536]{2,1,0:T(8,128)(2,1)S(1)}, bf16[32,48,512]{2,1,0:T(8,128)(2,1)S(1)}, bf16[32,32,512]{2,1,0:T(8,128)(2,1)S(1)}) custom-call(s32[8,128]{1,0:T(8,128)S(1)} %broadcast_in_dim.8.seg_ref, s32[128,128]{1,0:T(8,128)S(1)} %broadcast_in_dim.9.segcol_ref, s32[128,128]{1,0:T(8,128)S(1)} %broadcast_in_dim.22.order_ref, ...), custom_call_target="tpu_custom_call" | custom-call | tf_op jit(solution)/shard_map/exchange/pallas_call | solution.py:225
  85.3 0.0 copy-start.3
  85.3 1.6 %copy-done.3 = bf16[8,128,1536]{2,1,0:T(8,128)(2,1)} copy-done((bf16[8,128,1536]{2,1,0:T(8,128)(2,1)}, bf16[8,128,1536]{2,1,0:T(8,128)(2,1)S(1)}, u32[]{:S(2)}) %copy-start.3) | copy-done | bytes 3145752
  86.9 1.7 %reshape.26 = f32[32,8,4,512]{3,2,1,0:T(4,128)} reshape(bf16[32,32,512]{2,1,0:T(8,128)(2,1)S(1)} %get-tuple-element.7) | data formatting | bytes 3145728 | tf_op jit(solution)/shard_map/convert_element_type | solution.py:370
  88.6 3.4 %copy.11 = f32[32,8,4,512]{3,2,0,1:T(4,128)} copy(f32[32,8,4,512]{3,2,1,0:T(4,128)} %reshape.26) | data formatting | bytes 4194304 | tf_op jit(solution)/shard_map/convert_element_type | solution.py:370
  92.0 3.0 %reshape.25 = f32[1024,512]{1,0:T(8,128)} reshape(f32[8,32,4,512]{3,2,1,0:T(4,128)} %bitcast.16) | data formatting | bytes 4194304 | tf_op jit(solution)/shard_map/convert_element_type | solution.py:370
  94.9 0.0 copy-start.4
  94.9 4.5 %subtract_convert_fusion.resid_ref = bf16[1024,512]{1,0:T(8,128)(2,1)S(1)} fusion(f32[1024,512]{1,0:T(8,128)} %reshape.25, bf16[1024,1536]{1,0:T(8,128)(2,1)} %bitcast.14, bf16[1536,512]{1,0:T(8,128)(2,1)S(1)} %bitcast.11), kind=kOutput, calls=%fused_computation.2 | convolution fusion | flops 1611661312 | bytes 7864320 | tf_op jit(solution)/shard_map/dot_general | solution.py:369
  99.4 0.0 copy-done.4
  99.4 1.8 %convolution_convert_fusion = bf16[1536,512]{1,0:T(8,128)(2,1)S(1)} fusion(bf16[1024,1536]{1,0:T(8,128)(2,1)S(1)} %bitcast.15, bf16[1024,512]{1,0:T(8,128)(2,1)S(1)} %subtract_convert_fusion.resid_ref), kind=kOutput, calls=%fused_computation | convolution fusion | flops 1611399168 | bytes 5767168 | tf_op jit(solution)/shard_map/dot_general | solution.py:371
  101.3 45.1 %share.1 = (bf16[128,1536]{1,0:T(8,128)(2,1)S(1)}, f32[48,4096]{1,0:T(8,128)S(1)}) custom-call(bf16[1024,512]{1,0:T(8,128)(2,1)S(1)} %subtract_convert_fusion.resid_ref, bf16[1536,512]{1,0:T(8,128)(2,1)S(1)} %bitcast.12, bf16[32,48,512]{2,1,0:T(8,128)(2,1)S(1)} %bitcast.13), custom_call_target="tpu_custom_call" | custom-call | tf_op jit(solution)/shard_map/share/pallas_call | solution.py:335
  146.4 0.7 copy.14
  147.1 0.9 copy.15
Async XLA Ops:
  3.8 1.2 copy-start
  5.0 1.0 copy-start.1
  6.0 1.0 copy-start.2
  85.3 1.7 %copy-start.3 = (bf16[8,128,1536]{2,1,0:T(8,128)(2,1)}, bf16[8,128,1536]{2,1,0:T(8,128)(2,1)S(1)}, u32[]{:S(2)}) copy-start(bf16[8,128,1536]{2,1,0:T(8,128)(2,1)S(1)} %get-tuple-element.5) | copy-start | bytes 9437188
  94.9 4.5 %copy-start.4 = (bf16[8,128,1536]{2,1,0:T(8,128)(2,1)S(1)}, bf16[8,128,1536]{2,1,0:T(8,128)(2,1)}, u32[]{:S(2)}) copy-start(bf16[8,128,1536]{2,1,0:T(8,128)(2,1)} %copy-done.3) | copy-start | bytes 9437188

commit v5 on v4

--- a/solution.py
+++ b/solution.py
@@ -145,7 +145,8 @@
     trans = (((1,), (1,)), ((), ()))
 
     @pl.loop(0, cols)
-    def _(c):
+    def _(step):
+        c = (step + my_col + 1) % cols
         g = (c * heads) // per_group
         kcol = pl.ds(pl.multiple_of(g * HD, HD), HD)
         vcol = pl.ds(pl.multiple_of((KVH + g) * HD, HD), HD)
@@ -158,7 +159,7 @@
             scores = scores * (HD ** -0.5) + bias
             top = jnp.max(scores, axis=1, keepdims=True)
             weights = jnp.exp(scores - top)
-            weights = (weights / jnp.sum(weights, axis=1, keepdims=True)).astype(jnp.bfloat16)
+            weights = (weights * (1.0 / jnp.sum(weights, axis=1, keepdims=True))).astype(jnp.bfloat16)
             made.append(jnp.dot(weights, values, preferred_element_type=jnp.float32).astype(jnp.bfloat16))
         teacher = jnp.concatenate(made, axis=1)
         ordered = jnp.dot(pick, teacher, preferred_element_type=jnp.float32)
@@ -172,7 +173,7 @@
             def _():
                 out_copy(peer, me).start()
 
-        @pl.when(c == cols // 2)
+        @pl.when(step == cols // 2)
         def _():
             hops(1)
 
@@ -365,9 +366,15 @@
     )
     band_rows = band_rows.reshape(cols * rows, ds)
     column = column.reshape(n * depth, width)
-    target = arrived.reshape(n, cols, each, width).transpose(1, 0, 2, 3).reshape(cols * rows, width)
+    place = jnp.arange(cols * rows, dtype=jnp.int32)
+    owner, source, r = place // rows, (place % rows) // each, place % each
+    wanted = source * (cols * each) + owner * each + r
+    turn = (wanted[:, None] == place[None, :]).astype(jnp.bfloat16)
+    target = jnp.dot(
+        turn, arrived.reshape(cols * rows, width), preferred_element_type=jnp.float32
+    )
     predicted = jnp.dot(band_rows, column, preferred_element_type=jnp.float32)
-    residual = (predicted - target.astype(jnp.float32)).astype(jnp.bfloat16)
+    residual = (predicted - target).astype(jnp.bfloat16)
     proj_part = lax.dot_general(
         band_rows, residual, (((0,), (0,)), ((), ())), preferred_element_type=jnp.float32
     ).astype(jnp.bfloat16)

time: 148 us -> 137 us (0.926)
  local copies, waits for them, and re-layouts: 16.6 us -> 6.96 us
    convert_element_type x3 -> x0, local copies, waits for them, and re-layouts: 8.02 us -> none  [local(): residual = (predicted - target.astype(jnp.float32)).astype(jnp.bfloat16)]
    dot_general x1, matrix products: 4.47 us -> 1.78 us  [local(): predicted = jnp.dot(band_rows, column, preferred_element_type=jnp.float32)]
    pallas_call x1, Pallas kernels: 45.1 us -> 47.7 us  [share(): pl.pallas_call(functools.partial(share_kernel, n, scale), out_shape=(jax....]
    pallas_call x1, Pallas kernels: 78.3 us -> 75.9 us  [exchange(): pl.pallas_call(functools.partial(reach_kernel, n), out_shape=(jax.ShapeDt...]
    unnamed x12 -> x8, local copies, waits for them, and re-layouts: 6.48 us -> 4.84 us
where the time goes in v5:
time: 137 us
  Pallas kernels  124 us (91%)
  local copies, waits for them, and re-layouts  6.96 us (5%)
  matrix products  4.93 us (4%)
    pallas_call x1, Pallas kernels, exchange(): pl.pallas_call(functools.partial(reach_kernel, n), out_shape=(jax.ShapeDt...  75.9 us
    pallas_call x1, Pallas kernels, share(): pl.pallas_call(functools.partial(share_kernel, n, scale), out_shape=(jax....  47.7 us
    unnamed x8, local copies, waits for them, and re-layouts  4.84 us

profile of v5, /device:TPU:0, one launch (start us, length us, event | category | flops | bytes accessed | tf_op | source)
XLA Modules:
  0.0 137.1 jit_solution(3880207443825808493)
XLA Ops:
  0.6 0.7 broadcast_in_dim.8.seg_ref
  1.3 0.7 broadcast_in_dim.11.order_ref
  2.0 0.7 broadcast_in_dim.9.segcol_ref
  2.8 1.0 pad_maximum_fusion.pairs_ref
  3.8 0.0 copy-start
  3.8 1.2 copy-done
  5.0 0.0 copy-start.1
  5.0 1.0 copy-done.1
  6.0 0.0 copy-start.2
  6.0 1.0 copy-done.2
  7.0 75.9 %exchange.1 = (bf16[8,128,1536]{2,1,0:T(8,128)(2,1)S(1)}, bf16[32,48,512]{2,1,0:T(8,128)(2,1)S(1)}, bf16[32,32,512]{2,1,0:T(8,128)(2,1)S(1)}) custom-call(s32[8,128]{1,0:T(8,128)S(1)} %broadcast_in_dim.8.seg_ref, s32[128,128]{1,0:T(8,128)S(1)} %broadcast_in_dim.9.segcol_ref, s32[128,128]{1,0:T(8,128)S(1)} %broadcast_in_dim.11.order_ref, ...), custom_call_target="tpu_custom_call" | custom-call | tf_op jit(solution)/shard_map/exchange/pallas_call | solution.py:226
  82.9 1.3 fusion
  84.2 1.8 %subtract_convert_fusion.resid_ref = bf16[1024,512]{1,0:T(8,128)(2,1)S(1)} fusion(f32[1024,512]{1,0:T(8,128)S(1)} %fusion, bf16[1024,1536]{1,0:T(8,128)(2,1)S(1)} %bitcast.13, bf16[1536,512]{1,0:T(8,128)(2,1)S(1)} %bitcast.10), kind=kOutput, calls=%fused_computation.3 | convolution fusion | flops 1611661312 | bytes 7864320 | tf_op jit(solution)/shard_map/dot_general | solution.py:376
  86.0 1.9 %convolution_convert_fusion = bf16[1536,512]{1,0:T(8,128)(2,1)S(1)} fusion(bf16[1024,1536]{1,0:T(8,128)(2,1)S(1)} %bitcast.14, bf16[1024,512]{1,0:T(8,128)(2,1)S(1)} %subtract_convert_fusion.resid_ref), kind=kOutput, calls=%fused_computation.2 | convolution fusion | flops 1611399168 | bytes 5767168 | tf_op jit(solution)/shard_map/dot_general | solution.py:378
  87.9 47.7 %share.1 = (bf16[128,1536]{1,0:T(8,128)(2,1)S(1)}, f32[48,4096]{1,0:T(8,128)S(1)}) custom-call(bf16[1024,512]{1,0:T(8,128)(2,1)S(1)} %subtract_convert_fusion.resid_ref, bf16[1536,512]{1,0:T(8,128)(2,1)S(1)} %bitcast.11, bf16[32,48,512]{2,1,0:T(8,128)(2,1)S(1)} %bitcast.12), custom_call_target="tpu_custom_call" | custom-call | tf_op jit(solution)/shard_map/share/pallas_call | solution.py:336
  135.5 0.7 copy.11
  136.3 0.9 copy.12
  (1 shorter events, 0.0 us)
Async XLA Ops:
  3.8 1.2 copy-start
  5.0 1.0 copy-start.1
  6.0 1.0 copy-start.2

commit v6 on v5

--- a/solution.py
+++ b/solution.py
@@ -167,15 +167,22 @@
 
         @pl.loop(0, bands)
         def _(b):
-            peer = b * cols + c
+            peer = ((my_band + 1 + b) % bands) * cols + c
 
             @pl.when(peer != me)
             def _():
                 out_copy(peer, me).start()
 
+        @pl.when(step == 1)
+        def _():
+            hops(1)
+
         @pl.when(step == cols // 2)
         def _():
-            hops(1)
+            for k in range(1, cols // 2):
+                place = 2 * ((chip + chips - k) % chips) + parity
+                row_copy(k, place).wait()
+                pass_copy(k, place, place).start()
 
     own[2].start()
 
@@ -183,10 +190,6 @@
     def _(i):
         hops(i)
 
-    for k in range(1, cols // 2):
-        place = 2 * ((chip + chips - k) % chips) + parity
-        row_copy(k, place).wait()
-        pass_copy(k, place, place).start()
     own[0].wait()
     own[2].wait()
 
@@ -220,7 +223,6 @@
     segcol = jnp.broadcast_to(segment_ids[:, None], (rows, HD))
     order = jnp.broadcast_to(send_order[0][:, None], (rows, HD))
     vmem = pl.BlockSpec(memory_space=pltpu.VMEM)
-    hbm = pl.BlockSpec(memory_space=pl.ANY)
     dma = pltpu.SemaphoreType.DMA
     bf16 = jnp.bfloat16
     return pl.pallas_call(
@@ -230,8 +232,8 @@
             jax.ShapeDtypeStruct((n, depth, width), bf16),
             jax.ShapeDtypeStruct((n, rows // bands, width), bf16),
         ),
-        in_specs=[vmem] * 5 + [hbm] * 2,
-        out_specs=(hbm, hbm, hbm),
+        in_specs=[vmem] * 7,
+        out_specs=(vmem, vmem, vmem),
         scratch_shapes=[
             pltpu.VMEM((REACH, rows, pairs.shape[1]), bf16),
             pltpu.VMEM((REACH, 8, rows), jnp.int32),
@@ -247,8 +249,8 @@
 
 
 def share_kernel(n, scale, resid_ref, column_ref, part_ref, grows_ref, gproj_ref,
-                 twin_out, twin_in, rows_out, rows_in, proj_in,
-                 twin_send, twin_recv, row_send, row_recv, proj_send, proj_recv, own_sem):
+                 twin_out, twin_in, rows_out, rows_in, sum_in, sum_out, fin_in, fin_out,
+                 twin_send, twin_recv, row_send, row_recv, sum_send, sum_recv, fin_send, fin_recv):
     me = lax.axis_index("seq")
     cols = COLS
     bands = n // cols
@@ -263,9 +265,37 @@
             src_ref=src, dst_ref=dst, send_sem=send, recv_sem=recv,
             device_id={"seq": peer}, device_id_type=MESH)
 
-    def proj_copy(k, place):
-        peer = (me + k) % n
-        return remote(part_ref.at[peer], proj_in.at[place], proj_send.at[k], proj_recv.at[place], peer)
+    def sum_copy(way, t):
+        peer = (me + n + (cols if way == 0 else -cols)) % n
+        return remote(sum_out.at[way, t], sum_in.at[way, t],
+                      sum_send.at[way, t], sum_recv.at[way, t], peer)
+
+    def fin_copy(k, place):
+        j = (col + k) % cols
+        return remote(fin_out.at[j], fin_in.at[place], fin_send.at[k], fin_recv.at[place],
+                      band * cols + j)
+
+    def slab(b):
+        return part_ref[pl.ds(b * cols, cols)].astype(jnp.float32)
+
+    def chain(step):
+        for way, t, more, start in (
+            (0, bands - 1 - step, bands - 1 - step > band, band == 0),
+            (1, step, step < band, band == bands - 1),
+        ):
+            @pl.when(more & start)
+            def _():
+                sum_out[way, t] = slab(t).astype(sum_out.dtype)
+
+            @pl.when(more & jnp.logical_not(start))
+            def _():
+                sum_copy(way, t).wait_recv()
+                total = slab(t) + sum_in[way, t].astype(jnp.float32)
+                sum_out[way, t] = total.astype(sum_out.dtype)
+
+            @pl.when(more)
+            def _():
+                sum_copy(way, t).start()
 
     def twin_copy(t):
         return remote(twin_out.at[t], twin_in.at[t], twin_send.at[t], twin_recv.at[t], twin)
@@ -288,16 +318,11 @@
 
     pl.semaphore_wait(barrier, n - 1)
 
-    @pl.loop(1, n)
-    def _(k):
-        proj_copy(k, me).start()
-
-    own = pltpu.make_async_copy(part_ref.at[me], proj_in.at[me], own_sem.at[0])
-    own.start()
     for k in range(1, cols // 2 + 1):
         t = (chip + k) % chips
         twin_out[t] = product(2 * t + 1 - parity).astype(jnp.bfloat16)
         twin_copy(t).start()
+    chain(0)
     for k in range(1, cols // 2 + 1):
         t = (chip + k) % chips
         part = product(2 * t + parity)
@@ -306,24 +331,50 @@
         if k < cols // 2:
             rows_out[k] = part.astype(jnp.bfloat16)
             row_copy(k, chip).start()
+    @pl.loop(1, bands - 1)
+    def _(step):
+        chain(step)
+
+    for way, there in ((0, band > 0), (1, band < bands - 1)):
+        @pl.when(there)
+        def _():
+            sum_copy(way, band).wait_recv()
+
+    @pl.when((band > 0) & (band < bands - 1))
+    def _():
+        fin_out[...] = (slab(band) + sum_in[0, band].astype(jnp.float32)
+                        + sum_in[1, band].astype(jnp.float32)).astype(jnp.bfloat16)
+
+    @pl.when(band == 0)
+    def _():
+        fin_out[...] = (slab(band) + sum_in[1, band].astype(jnp.float32)).astype(jnp.bfloat16)
+
+    @pl.when((band > 0) & (band == bands - 1))
+    def _():
+        fin_out[...] = (slab(band) + sum_in[0, band].astype(jnp.float32)).astype(jnp.bfloat16)
+
+    fin_in[col] = fin_out[col]
+    for k in range(1, cols):
+        fin_copy(k, col).start()
     for k in range(1, cols // 2):
         place = (chip + chips - k) % chips
         row_copy(k, place).wait()
         part = part + rows_in[place].astype(jnp.float32)
     grows_ref[...] = part.astype(jnp.bfloat16)
-    own.wait()
-
-    @pl.loop(1, n)
-    def _(k):
-        proj_copy(k, (me + n - k) % n).wait()
-
-    @pl.loop(0, cols)
-    def _(c):
-        def add(b, total):
-            return total + proj_in[b * cols + c].astype(jnp.float32)
-
-        total = lax.fori_loop(1, bands, add, proj_in[c].astype(jnp.float32))
-        gproj_ref[:, pl.ds(pl.multiple_of(c * width, width), width)] = total * scale
+    for k in range(1, cols):
+        fin_copy(k, (col + cols - k) % cols).wait()
+    for c in range(cols):
+        gproj_ref[:, c * width : (c + 1) * width] = fin_in[c].astype(jnp.float32) * scale
+
+    @pl.loop(0, bands)
+    def _(t):
+        @pl.when((t > band))
+        def _():
+            sum_copy(0, t).wait_send()
+
+        @pl.when((t < band))
+        def _():
+            sum_copy(1, t).wait_send()
 
 
 def share(residual, column, parts, rows, scale):
@@ -333,17 +384,22 @@
     dma = pltpu.SemaphoreType.DMA
     bf16 = jnp.bfloat16
     half = COLS // 2
+    wire = bf16 if n // COLS <= 4 else jnp.float32
     return pl.pallas_call(
         functools.partial(share_kernel, n, scale),
         out_shape=(
             jax.ShapeDtypeStruct((rows, ds), bf16),
             jax.ShapeDtypeStruct((depth, COLS * width), jnp.float32),
         ),
-        in_specs=[vmem] * 2 + [pl.BlockSpec(memory_space=pl.ANY)],
+        in_specs=[vmem] * 3,
         out_specs=(vmem, vmem),
         scratch_shapes=[pltpu.VMEM((half, rows, ds), bf16)] * 4 + [
-            pltpu.VMEM((n, depth, width), bf16),
-            dma((half,)), dma((half,)), dma((half,)), dma((half,)), dma((n,)), dma((n,)), dma((1,)),
+            pltpu.VMEM((2, n // COLS, COLS, depth, width), wire),
+            pltpu.VMEM((2, n // COLS, COLS, depth, width), wire),
+            pltpu.VMEM((COLS, depth, width), bf16),
+            pltpu.VMEM((COLS, depth, width), bf16),
+            dma((half,)), dma((half,)), dma((half,)), dma((half,)),
+            dma((2, n // COLS)), dma((2, n // COLS)), dma((COLS,)), dma((COLS,)),
         ],
         compiler_params=pltpu.CompilerParams(
             collective_id=1, has_side_effects=True, vmem_limit_bytes=40 * 1024 * 1024),

time: 137 us -> 144 us (1.051)
  the two profiles are of different devices: /device:TPU:0 before, /device:TPU:9 now
where the time goes in v6:
time: 144 us
  Pallas kernels  130 us (90%)
  local copies, waits for them, and re-layouts  6.96 us (5%)
  matrix products  4.95 us (3%)
    pallas_call x1, Pallas kernels, exchange(): pl.pallas_call(functools.partial(reach_kernel, n), out_shape=(jax.ShapeDt...  69.7 us
    pallas_call x1, Pallas kernels, share(): pl.pallas_call(functools.partial(share_kernel, n, scale), out_shape=(jax....  60.7 us
    unnamed x8, local copies, waits for them, and re-layouts  4.84 us

profile of v6, /device:TPU:9, one launch (start us, length us, event | category | flops | bytes accessed | tf_op | source)
XLA Modules:
  0.0 144.0 jit_solution(13075053177350614112)
XLA Ops:
  0.6 0.7 broadcast_in_dim.8.seg_ref
  1.3 0.7 broadcast_in_dim.11.order_ref
  2.0 0.7 broadcast_in_dim.9.segcol_ref
  2.8 1.0 pad_maximum_fusion.pairs_ref
  3.8 0.0 copy-start
  3.8 1.2 copy-done
  5.0 0.0 copy-start.1
  5.0 1.0 copy-done.1
  6.0 0.0 copy-start.2
  6.0 1.0 copy-done.2
  7.0 69.7 %exchange.1 = (bf16[8,128,1536]{2,1,0:T(8,128)(2,1)S(1)}, bf16[32,48,512]{2,1,0:T(8,128)(2,1)S(1)}, bf16[32,32,512]{2,1,0:T(8,128)(2,1)S(1)}) custom-call(s32[8,128]{1,0:T(8,128)S(1)} %broadcast_in_dim.8.seg_ref, s32[128,128]{1,0:T(8,128)S(1)} %broadcast_in_dim.9.segcol_ref, s32[128,128]{1,0:T(8,128)S(1)} %broadcast_in_dim.11.order_ref, ...), custom_call_target="tpu_custom_call" | custom-call | tf_op jit(solution)/shard_map/exchange/pallas_call | solution.py:228
  76.7 1.3 fusion
  78.0 1.8 %subtract_convert_fusion.resid_ref = bf16[1024,512]{1,0:T(8,128)(2,1)S(1)} fusion(f32[1024,512]{1,0:T(8,128)S(1)} %fusion, bf16[1024,1536]{1,0:T(8,128)(2,1)S(1)} %bitcast.13, bf16[1536,512]{1,0:T(8,128)(2,1)S(1)} %bitcast.10), kind=kOutput, calls=%fused_computation.3 | convolution fusion | flops 1611661312 | bytes 7864320 | tf_op jit(solution)/shard_map/dot_general | solution.py:432
  79.8 1.9 %convolution_convert_fusion = bf16[1536,512]{1,0:T(8,128)(2,1)S(1)} fusion(bf16[1024,1536]{1,0:T(8,128)(2,1)S(1)} %bitcast.14, bf16[1024,512]{1,0:T(8,128)(2,1)S(1)} %subtract_convert_fusion.resid_ref), kind=kOutput, calls=%fused_computation.2 | convolution fusion | flops 1611399168 | bytes 5767168 | tf_op jit(solution)/shard_map/dot_general | solution.py:434
  81.7 60.7 %share.1 = (bf16[128,1536]{1,0:T(8,128)(2,1)S(1)}, f32[48,4096]{1,0:T(8,128)S(1)}) custom-call(bf16[1024,512]{1,0:T(8,128)(2,1)S(1)} %subtract_convert_fusion.resid_ref, bf16[1536,512]{1,0:T(8,128)(2,1)S(1)} %bitcast.11, bf16[32,48,512]{2,1,0:T(8,128)(2,1)S(1)} %bitcast.12), custom_call_target="tpu_custom_call" | custom-call | tf_op jit(solution)/shard_map/share/pallas_call | solution.py:388
  142.4 0.7 copy.11
  143.1 0.9 copy.12
  (1 shorter events, 0.0 us)
Async XLA Ops:
  3.8 1.2 copy-start
  5.0 1.0 copy-start.1
  6.0 1.0 copy-start.2

commit v7 on v5

--- a/solution.py
+++ b/solution.py
@@ -167,15 +167,22 @@
 
         @pl.loop(0, bands)
         def _(b):
-            peer = b * cols + c
+            peer = ((my_band + 1 + b) % bands) * cols + c
 
             @pl.when(peer != me)
             def _():
                 out_copy(peer, me).start()
 
+        @pl.when(step == 1)
+        def _():
+            hops(1)
+
         @pl.when(step == cols // 2)
         def _():
-            hops(1)
+            for k in range(1, cols // 2):
+                place = 2 * ((chip + chips - k) % chips) + parity
+                row_copy(k, place).wait()
+                pass_copy(k, place, place).start()
 
     own[2].start()
 
@@ -183,10 +190,6 @@
     def _(i):
         hops(i)
 
-    for k in range(1, cols // 2):
-        place = 2 * ((chip + chips - k) % chips) + parity
-        row_copy(k, place).wait()
-        pass_copy(k, place, place).start()
     own[0].wait()
     own[2].wait()
 
@@ -220,7 +223,6 @@
     segcol = jnp.broadcast_to(segment_ids[:, None], (rows, HD))
     order = jnp.broadcast_to(send_order[0][:, None], (rows, HD))
     vmem = pl.BlockSpec(memory_space=pltpu.VMEM)
-    hbm = pl.BlockSpec(memory_space=pl.ANY)
     dma = pltpu.SemaphoreType.DMA
     bf16 = jnp.bfloat16
     return pl.pallas_call(
@@ -230,8 +232,8 @@
             jax.ShapeDtypeStruct((n, depth, width), bf16),
             jax.ShapeDtypeStruct((n, rows // bands, width), bf16),
         ),
-        in_specs=[vmem] * 5 + [hbm] * 2,
-        out_specs=(hbm, hbm, hbm),
+        in_specs=[vmem] * 7,
+        out_specs=(vmem, vmem, vmem),
         scratch_shapes=[
             pltpu.VMEM((REACH, rows, pairs.shape[1]), bf16),
             pltpu.VMEM((REACH, 8, rows), jnp.int32),
@@ -339,7 +341,7 @@
             jax.ShapeDtypeStruct((rows, ds), bf16),
             jax.ShapeDtypeStruct((depth, COLS * width), jnp.float32),
         ),
-        in_specs=[vmem] * 2 + [pl.BlockSpec(memory_space=pl.ANY)],
+        in_specs=[vmem] * 3,
         out_specs=(vmem, vmem),
         scratch_shapes=[pltpu.VMEM((half, rows, ds), bf16)] * 4 + [
             pltpu.VMEM((n, depth, width), bf16),

time: 137 us -> 135 us (0.985)
  Pallas kernels: 124 us -> 121 us
    pallas_call x1, Pallas kernels: 75.9 us -> 69.4 us  [exchange(): pl.pallas_call(functools.partial(reach_kernel, n), out_shape=(jax.ShapeDt...]
    pallas_call x1, Pallas kernels: 47.7 us -> 51.6 us  [share(): pl.pallas_call(functools.partial(share_kernel, n, scale), out_shape=(jax....]
where the time goes in v7:
time: 135 us
  Pallas kernels  121 us (90%)
  local copies, waits for them, and re-layouts  6.96 us (5%)
  matrix products  4.94 us (4%)
    pallas_call x1, Pallas kernels, exchange(): pl.pallas_call(functools.partial(reach_kernel, n), out_shape=(jax.ShapeDt...  69.4 us
    pallas_call x1, Pallas kernels, share(): pl.pallas_call(functools.partial(share_kernel, n, scale), out_shape=(jax....  51.6 us
    unnamed x8, local copies, waits for them, and re-layouts  4.84 us

profile of v7, /device:TPU:0, one launch (start us, length us, event | category | flops | bytes accessed | tf_op | source)
XLA Modules:
  0.0 134.6 jit_solution(6179699673925772863)
XLA Ops:
  0.6 0.7 broadcast_in_dim.8.seg_ref
  1.3 0.7 broadcast_in_dim.11.order_ref
  2.0 0.7 broadcast_in_dim.9.segcol_ref
  2.8 1.0 pad_maximum_fusion.pairs_ref
  3.8 0.0 copy-start
  3.8 1.2 copy-done
  5.0 0.0 copy-start.1
  5.0 1.0 copy-done.1
  6.0 0.0 copy-start.2
  6.0 1.0 copy-done.2
  7.0 69.4 %exchange.1 = (bf16[8,128,1536]{2,1,0:T(8,128)(2,1)S(1)}, bf16[32,48,512]{2,1,0:T(8,128)(2,1)S(1)}, bf16[32,32,512]{2,1,0:T(8,128)(2,1)S(1)}) custom-call(s32[8,128]{1,0:T(8,128)S(1)} %broadcast_in_dim.8.seg_ref, s32[128,128]{1,0:T(8,128)S(1)} %broadcast_in_dim.9.segcol_ref, s32[128,128]{1,0:T(8,128)S(1)} %broadcast_in_dim.11.order_ref, ...), custom_call_target="tpu_custom_call" | custom-call | tf_op jit(solution)/shard_map/exchange/pallas_call | solution.py:228
  76.4 1.3 fusion
  77.7 1.8 %subtract_convert_fusion.resid_ref = bf16[1024,512]{1,0:T(8,128)(2,1)S(1)} fusion(f32[1024,512]{1,0:T(8,128)S(1)} %fusion, bf16[1024,1536]{1,0:T(8,128)(2,1)S(1)} %bitcast.13, bf16[1536,512]{1,0:T(8,128)(2,1)S(1)} %bitcast.10), kind=kOutput, calls=%fused_computation.3 | convolution fusion | flops 1611661312 | bytes 7864320 | tf_op jit(solution)/shard_map/dot_general | solution.py:378
  79.5 1.9 %convolution_convert_fusion = bf16[1536,512]{1,0:T(8,128)(2,1)S(1)} fusion(bf16[1024,1536]{1,0:T(8,128)(2,1)S(1)} %bitcast.14, bf16[1024,512]{1,0:T(8,128)(2,1)S(1)} %subtract_convert_fusion.resid_ref), kind=kOutput, calls=%fused_computation.2 | convolution fusion | flops 1611399168 | bytes 5767168 | tf_op jit(solution)/shard_map/dot_general | solution.py:380
  81.4 51.6 %share.1 = (bf16[128,1536]{1,0:T(8,128)(2,1)S(1)}, f32[48,4096]{1,0:T(8,128)S(1)}) custom-call(bf16[1024,512]{1,0:T(8,128)(2,1)S(1)} %subtract_convert_fusion.resid_ref, bf16[1536,512]{1,0:T(8,128)(2,1)S(1)} %bitcast.11, bf16[32,48,512]{2,1,0:T(8,128)(2,1)S(1)} %bitcast.12), custom_call_target="tpu_custom_call" | custom-call | tf_op jit(solution)/shard_map/share/pallas_call | solution.py:338
  132.9 0.7 copy.11
  133.7 0.9 copy.12
  (1 shorter events, 0.0 us)
Async XLA Ops:
  3.8 1.2 copy-start
  5.0 1.0 copy-start.1
  6.0 1.0 copy-start.2
